TPU v7x, 32 devices: a whole 2x2x4 slice. The times are simulated.
32 devices in a mesh: pole: 2 (over y), row: 4 (over z), col: 4 (over x, core).
Axes of the slice: x: 2, y: 2, z: 4, core: 2. Of those that a mesh axis runs over, the one named last changes fastest.
Arguments:
- front_h: bfloat16 [1024, 1024], P(('row', 'col')), may hold values from -6 to 6
- front_s: bfloat16 [1024, 1024], P(('row', 'col')), may hold values from -6 to 6
- panel_h: bfloat16 [1024, 256], P('row'), may hold values from -6 to 6
- panel_s: bfloat16 [1024, 256], P('row'), may hold values from -4 to 4
- pivot_h: bfloat16 [256, 256], replicated, may hold values from -1.7 to 8.5, as said below
- pivot_s: bfloat16 [256, 256], replicated, may hold values from -0.1 to 1.5, as said below
- pole_shift: float32 [2, 2], P('pole'), may hold values from -0.5 to 1.5, as said below
- pole_weight: float32 [2, 2], P('pole'), may hold values from -6 to 6
- pattern: int32 [4, 4], replicated, may hold values 0 or 1
- ancestor_inverse: bfloat16 [2, 2, 4, 4, 64, 1024], P('pole', None, None, 'col', None, 'row'), may hold values from -0.1875 to 0.1875
Outputs:
- schur: bfloat16 [2, 2, 4, 4, 64, 1024], P('pole', None, None, 'col', None, 'row')
- density_rows: float32 [1024, 256], P(('row', 'col'), 'pole')
- density_pivot: float32 [256, 256], P(None, 'pole')
Inputs may be any that keep to these rules, and one draw needn't show every extreme that they name: `pivot_h`: symmetric; each row's off-diagonal entries sum in magnitude to at most 6.6, the diagonal lies in 8 to 8.5. `pivot_s`: symmetric; each row's off-diagonal entries sum in magnitude to at most 0.33, the diagonal lies in 1 to 1.5. `pole_shift`: column 0 lies in -0.5 to 0.5, column 1 in 0.25 to 1.5.
All inputs are finite; a program needn't handle non-finite values.
Results may differ from a plain program's by a relative error of at most 0.0063.
Values may be sent and summed in bfloat16 or wider, within the bound.
A program may use at most 64 MiB of HBM per device.

v0:
```python
import jax
import jax.numpy as jnp
from jax import lax
from jax.sharding import PartitionSpec as P

NEWTON = 4


highest = lax.Precision.HIGHEST


def complex_matmul(left_real, left_imag, right_real, right_imag):
    real = jnp.dot(
        left_real, right_real, precision=highest, preferred_element_type=jnp.float32
    ) - jnp.dot(left_imag, right_imag, precision=highest, preferred_element_type=jnp.float32)
    imag = jnp.dot(
        left_real, right_imag, precision=highest, preferred_element_type=jnp.float32
    ) + jnp.dot(left_imag, right_real, precision=highest, preferred_element_type=jnp.float32)
    return (real, imag)


def complex_einsum(form, left_real, left_imag, right_real, right_imag, accurate):
    if accurate:
        real = jnp.einsum(form, left_real, right_real, precision=highest) - jnp.einsum(
            form, left_imag, right_imag, precision=highest
        )
        imag = jnp.einsum(form, left_real, right_imag, precision=highest) + jnp.einsum(
            form, left_imag, right_real, precision=highest
        )
    else:
        real = jnp.einsum(
            form, left_real, right_real, preferred_element_type=jnp.float32
        ) - jnp.einsum(form, left_imag, right_imag, preferred_element_type=jnp.float32)
        imag = jnp.einsum(
            form, left_real, right_imag, preferred_element_type=jnp.float32
        ) + jnp.einsum(form, left_imag, right_real, preferred_element_type=jnp.float32)
    return (real, imag)


def invert_pivot(pivot_h, pivot_s, shift_real, shift_imag, sweeps):
    matrix_real = pivot_h.astype(jnp.float32) - shift_real * pivot_s.astype(jnp.float32)
    matrix_imag = -shift_imag * pivot_s.astype(jnp.float32)
    diag_real = jnp.diagonal(matrix_real)
    diag_imag = jnp.diagonal(matrix_imag)
    denom = diag_real * diag_real + diag_imag * diag_imag
    identity = jnp.eye(matrix_real.shape[0], dtype=jnp.float32)

    def advance(index, state):
        approx_real, approx_imag = state
        prod_real, prod_imag = complex_matmul(matrix_real, matrix_imag, approx_real, approx_imag)
        return complex_matmul(approx_real, approx_imag, 2.0 * identity - prod_real, -prod_imag)

    start = (jnp.diag(diag_real / denom), jnp.diag(-diag_imag / denom))
    return lax.fori_loop(0, sweeps, advance, start)


def solve_rows(rows_h, rows_s, shift_real, shift_imag, inv_real, inv_imag):
    coupled_real = (rows_h.astype(jnp.float32) - shift_real * rows_s.astype(jnp.float32)).astype(
        jnp.bfloat16
    )
    coupled_imag = (-shift_imag * rows_s.astype(jnp.float32)).astype(jnp.bfloat16)
    result_real, result_imag = complex_matmul(
        coupled_real.astype(jnp.float32), coupled_imag.astype(jnp.float32), inv_real, inv_imag
    )
    return (coupled_real, coupled_imag, jnp.stack([result_real, result_imag]).astype(jnp.bfloat16))


def shards(
    front_h,
    front_s,
    panel_h,
    panel_s,
    pivot_h,
    pivot_s,
    pole_shift,
    pole_weight,
    pattern,
    ancestor_inverse,
):
    row_count = lax.axis_size("row")
    col_count = lax.axis_size("col")
    pole_count = lax.axis_size("pole")
    row_index = lax.axis_index("row")
    col_index = lax.axis_index("col")
    shift_real = pole_shift[0, 0]
    shift_imag = pole_shift[0, 1]
    weight_real = pole_weight[0, 0]
    weight_imag = pole_weight[0, 1]
    supernode = pivot_h.shape[0]
    piece = supernode // pole_count
    hamil_cols, margin_cols = (
        lax.all_to_all(front_h, "row", split_axis=1, concat_axis=0, tiled=True),
        lax.all_to_all(front_s, "row", split_axis=1, concat_axis=0, tiled=True),
    )
    width = hamil_cols.shape[0] // row_count
    block_rows = hamil_cols.shape[1]
    local_cols = jnp.arange(row_count * width)
    global_cols = (local_cols // width * col_count + col_index) * width + local_cols % width
    global_rows = row_index * block_rows + jnp.arange(block_rows)
    tile_mask = jnp.take(
        jnp.take(pattern, global_cols // supernode, axis=0), global_rows // supernode, axis=1
    ).astype(jnp.float32)
    margin_f = margin_cols.astype(jnp.float32)
    front_real = tile_mask * (hamil_cols.astype(jnp.float32) - shift_real * margin_f)
    front_imag = tile_mask * (-shift_imag * margin_f)
    inv_real, inv_imag = invert_pivot(pivot_h, pivot_s, shift_real, shift_imag, NEWTON)
    coupling_real, coupling_imag, solved = solve_rows(
        panel_h, panel_s, shift_real, shift_imag, inv_real, inv_imag
    )
    solved_strip = lax.dynamic_slice_in_dim(solved, col_index * width, width, axis=1)
    far_solved = lax.all_gather(solved_strip, "row", axis=1, tiled=True)
    update_real, update_imag = complex_einsum(
        "gk,ik->gi", far_solved[0], far_solved[1], coupling_real, coupling_imag, False
    )
    schur = jnp.stack([front_real - update_real, front_imag - update_imag]).astype(jnp.bfloat16)
    schur = schur.reshape(1, 2, row_count, 1, width, block_rows)
    ancestor = ancestor_inverse.reshape(2, row_count * width, block_rows)
    part_real, part_imag = complex_einsum(
        "gi,gk->ik", ancestor[0], ancestor[1], far_solved[0], far_solved[1], False
    )
    column = lax.psum_scatter(
        jnp.stack([-part_real, -part_imag]), "col", scatter_dimension=1, tiled=True
    )
    strip_f = solved_strip.astype(jnp.float32)
    corr_real, corr_imag = complex_einsum(
        "sk,sl->kl", strip_f[0], strip_f[1], column[0], column[1], True
    )
    correction = lax.psum(jnp.stack([corr_real, corr_imag]), ("row", "col"))
    rows_ready = weight_real * column[1] + weight_imag * column[0]
    block_real = inv_real - correction[0]
    block_imag = inv_imag - correction[1]
    pivot_density = weight_real * block_imag + weight_imag * block_real
    pole_items = (rows_ready, pivot_density)
    start_col = lax.axis_index("pole") * piece
    summed = lax.psum((pole_items[0], pole_items[1]), "pole")
    shares = tuple(
        (lax.dynamic_slice_in_dim(member, start_col, piece, axis=1) for member in summed)
    )
    rows_out = shares[0]
    pivot_out = shares[1]
    return (schur, rows_out, pivot_out)


def solution(mesh):
    in_specs = (
        P(("row", "col"), None),
        P(("row", "col"), None),
        P("row", None),
        P("row", None),
        P(),
        P(),
        P("pole", None),
        P("pole", None),
        P(),
        P("pole", None, None, "col", None, "row"),
    )
    out_specs = (
        P("pole", None, None, "col", None, "row"),
        P(("row", "col"), "pole"),
        P(None, "pole"),
    )
    return jax.shard_map(shards, mesh=mesh, in_specs=in_specs, out_specs=out_specs, check_vma=False)
```

profile of v0, /device:TPU:0, one launch (start us, length us, event | category | flops | bytes accessed | tf_op | source)
XLA Modules:
  0.0 217.3 jit_solution(6498196070532619226)
XLA Ops:
  9.1 1.8 convert_multiply_fusion
  10.9 2.3 %gather_fusion.2 = f32[256]{0:T(256)S(1)} fusion(f32[256,256]{1,0:T(8,128)S(1)} %get-tuple-element.121, s32[256]{0:T(256)S(1)} %bitcast.169), kind=kCustom, calls=%fused_computation.2 | custom fusion | bytes 4096 | tf_op jit(solution)/shard_map/jit(diagonal)/cond/branch_0_fun/gather | solution.py:43
  13.3 2.3 %gather_fusion.3 = f32[256]{0:T(256)S(1)} fusion(f32[256,256]{1,0:T(8,128)S(1)} %get-tuple-element.122, s32[256]{0:T(256)S(1)} %bitcast.170), kind=kCustom, calls=%fused_computation.3 | custom fusion | bytes 4096 | tf_op jit(solution)/shard_map/jit(diagonal)/cond/branch_0_fun/gather | solution.py:44
  15.7 16.6 %while.13 = (s32[]{:T(128)}, f32[256,256]{0,1:T(8,128)S(1)}, f32[256,256]{0,1:T(8,128)S(1)}, f32[256,256]{1,0:T(8,128)S(1)}, f32[256,256]{1,0:T(8,128)S(1)}, /*index=5*/s32[]{:T(128)}) while((s32[]{:T(128)}, f32[256,256]{0,1:T(8,128)S(1)}, f32[256,256]{0,1:T(8,128)S(1)}, f32[256,256]{1,0:T(8,128)S(1)}, f32[256,256]{1,0:T(8,128)S(1)}, ...), condition=%wide.region_1.2_spmd.clone, body=%wide.region_0.1_spmd.clone.sunk | while | flops 1611137024 | bytes 7864389 | solution.py:54
  34.2 15.8 %all_gather.3 = bf16[2,256,256]{2,1,0:T(8,128)(2,1)S(1)} all-gather(bf16[2,64,256]{2,1,0:T(8,128)(2,1)S(1)} %fusion.40), channel_id=1, replica_groups=mesh['pole'=2,'row'=4,'col'=4] {'row'}, dimensions={1}, use_global_device_ids=true | all-gather | bytes 327680 | tf_op jit(solution)/shard_map/all_gather | solution.py:111
  51.0 1.0 copy.37
  52.0 0.9 copy-done.3
  52.9 0.7 copy.62
  53.5 5.2 %all-to-all-start = ((bf16[64,4,256]{2,0,1:T(8,128)(2,1)}), bf16[64,4,256]{2,0,1:T(8,128)(2,1)S(1)}, u32[]{:S(2)}, u32[]{:S(2)}) async-start(bf16[64,4,256]{2,0,1:T(8,128)(2,1)} %bitcast.132), calls=%async_computation | async-start | bytes 262144 | tf_op jit(solution)/shard_map/all_to_all | solution.py:92
  60.4 0.7 gather_fusion
  61.3 1.0 gather_fusion.1
  62.4 0.8 copy-done.4
  66.0 5.1 %all-to-all-start.1 = ((bf16[64,4,256]{2,0,1:T(8,128)(2,1)}), bf16[64,4,256]{2,0,1:T(8,128)(2,1)S(1)}, u32[]{:S(2)}, u32[]{:S(2)}) async-start(bf16[64,4,256]{2,0,1:T(8,128)(2,1)} %bitcast.131), calls=%async_computation.1 | async-start | bytes 262144 | tf_op jit(solution)/shard_map/all_to_all | solution.py:93
  71.3 5.7 %all-to-all-done.1 = bf16[64,4,256]{2,0,1:T(8,128)(2,1)S(1)} async-done(((bf16[64,4,256]{2,0,1:T(8,128)(2,1)}), bf16[64,4,256]{2,0,1:T(8,128)(2,1)S(1)}, u32[]{:S(2)}, u32[]{:S(2)}) %all-to-all-start.1) | async-done | bytes 131104 | tf_op jit(solution)/shard_map/all_to_all | solution.py:93
  77.0 0.7 fusion.20
  77.8 9.1 %all-reduce.8.cloned.1.call-done = f32[2,256,256]{2,0,1:T(2,128)} async-done(((f32[2,256,256]{2,0,1:T(2,128)}), f32[2,256,256]{2,0,1:T(2,128)}) %all-reduce.8.cloned.1.call-update) | async-done | bytes 524304
  86.9 1.1 constant_dynamic-slice_fusion.3
  89.2 0.8 pad_maximum_fusion.1
  90.4 1.9 fusion.44
  92.3 88.1 %all-reduce.6.cloned.1.call-done = f32[2,256,256]{2,1,0:T(8,128)} async-done(((f32[2,256,256]{2,1,0:T(8,128)}), f32[2,256,256]{2,1,0:T(8,128)}) %all-reduce.6.cloned.1.call-update) | async-done | bytes 524304 | tf_op jit(solution)/shard_map/psum | solution.py:128
  180.4 3.1 %fusion.27 = f32[256,256]{1,0:T(8,128)} fusion(f32[256,256]{1,0:T(8,128)S(1)} %copy.40, f32[2,256,256]{2,1,0:T(8,128)} %all-reduce.6.cloned.1.call-done, f32[256,256]{1,0:T(8,128)S(1)} %copy.39, f32[]{:T(128)} %bitcast.26, f32[]{:T(128)} %bitcast.18), kind=kLoop, calls=%fused_computation.52 | loop fusion | flops 327680 | bytes 1310728 | tf_op jit(solution)/shard_map/add | solution.py:132
  183.7 0.7 pad_maximum_fusion.2
  184.4 24.2 %all-reduce.10.cloned.1.call-done = (f32[64,256]{1,0:T(8,128)}, f32[256,256]{1,0:T(8,128)}) async-done(((f32[64,256]{1,0:T(8,128)}, f32[256,256]{1,0:T(8,128)}), (f32[64,256]{1,0:T(8,128)}, f32[256,256]{1,0:T(8,128)})) %all-reduce.10.cloned.1.call-update) | async-done | bytes 327696 | tf_op jit(solution)/shard_map/psum | solution.py:135
  208.6 1.6 constant_dynamic-slice_fusion
  (98 shorter events, 27.1 us)
Async XLA Ops:
  7.2 53.2 %copy-start = (s32[4,4]{1,0:T(4,128)S(1)}, s32[4,4]{1,0:T(4,128)}, u32[]{:S(2)}) copy-start(s32[4,4]{1,0:T(4,128)} %param.20) | copy-start | bytes 196
  7.2 0.7 copy-start.6
  7.2 79.7 %all-reduce.8.cloned.1.call-start = ((), (), s32[]{:S(2)}) async-start(), calls=%async_computation.3 | async-start | bytes 1048576
  32.6 0.9 copy-start.1
  34.2 15.8 %copy-start.2 = (bf16[1,2,4,1,64,256]{5,4,3,2,1,0:T(8,128)(2,1)S(1)}, bf16[1,2,4,1,64,256]{5,4,3,2,1,0:T(8,128)(2,1)}, u32[]{:S(2)}) copy-start(bf16[1,2,4,1,64,256]{5,4,3,2,1,0:T(8,128)(2,1)} %param.21) | copy-start | bytes 786436
  52.0 0.9 copy-start.3
  53.5 12.4 %all-to-all-start = ((bf16[64,4,256]{2,0,1:T(8,128)(2,1)}), bf16[64,4,256]{2,0,1:T(8,128)(2,1)S(1)}, u32[]{:S(2)}, u32[]{:S(2)}) async-start(bf16[64,4,256]{2,0,1:T(8,128)(2,1)} %bitcast.132), calls=%async_computation | async-start | bytes 262144 | tf_op jit(solution)/shard_map/all_to_all | solution.py:92
  59.0 0.7 copy-start.7
  62.3 0.9 copy-start.4
  63.8 0.7 copy-start.8
  66.0 11.0 %all-to-all-start.1 = ((bf16[64,4,256]{2,0,1:T(8,128)(2,1)}), bf16[64,4,256]{2,0,1:T(8,128)(2,1)S(1)}, u32[]{:S(2)}, u32[]{:S(2)}) async-start(bf16[64,4,256]{2,0,1:T(8,128)(2,1)} %bitcast.131), calls=%async_computation.1 | async-start | bytes 262144 | tf_op jit(solution)/shard_map/all_to_all | solution.py:93
  71.1 109.3 %all-reduce.6.cloned.1.call-start = ((), (), s32[]{:S(2)}) async-start(), calls=%async_computation.2 | async-start | bytes 1048576 | tf_op jit(solution)/shard_map/psum | solution.py:128
  90.1 118.5 %all-reduce.10.cloned.1.call-start = ((), (), s32[]{:S(2)}) async-start(), calls=%async_computation.4 | async-start | bytes 655360 | tf_op jit(solution)/shard_map/psum | solution.py:135
  208.6 1.6 copy-start.5
Sparse Core Ops, SparseCore 0:
  52.1 34.6 all-reduce.7
  90.3 90.0 all-reduce.5
  183.6 24.9 all-reduce.9
where the time goes:
time: 218 us; the launch traced here: 217 us
  waiting for transfers between devices  127 us (58%)
  matrix products  20.5 us (9%)
  local copies, waits for them, and re-layouts  18.6 us (9%)
  blocking collectives  15.8 us (7%)
  between operations  15.4 us (7%)
  starting transfers between devices  10.3 us (5%)
  other arithmetic  9.35 us (4%)
    psum x1, waiting for transfers between devices, shards(): correction = lax.psum(jnp.stack([corr_real, corr_imag]), ('row', 'col'))  88.1 us
    psum x1, waiting for transfers between devices, shards(): summed = lax.psum((pole_items[0], pole_items[1]), 'pole')  24.2 us
    all_gather x1, blocking collectives, shards(): far_solved = lax.all_gather(solved_strip, 'row', axis=1, tiled=True)  15.8 us
    unnamed x4, waiting for transfers between devices  9.15 us
    all_to_all x1, waiting for transfers between devices, shards(): lax.all_to_all(front_s, 'row', split_axis=1, concat_axis=0, tiled=True)  5.7 us
    all_to_all x1, starting transfers between devices, shards(): lax.all_to_all(front_h, 'row', split_axis=1, concat_axis=0, tiled=True)  5.16 us
    all_to_all x1, starting transfers between devices, shards(): lax.all_to_all(front_s, 'row', split_axis=1, concat_axis=0, tiled=True)  5.1 us
    unnamed x19, local copies, waits for them, and re-layouts  4.75 us
  transfers between devices with their start and end apart: 5, of which 4 were waited for; matrix products, arithmetic and copies ran while one was open for 4% of the time, Pallas kernels for 0%

commit v1 on v0

v1 whole, which is shorter than its diff:
```python
import functools

import jax
import jax.numpy as jnp
from jax import lax
from jax.experimental import pallas as pl
from jax.experimental.pallas import tpu as pltpu
from jax.sharding import PartitionSpec as P

MESH = pl.DeviceIdType.MESH
F32 = jnp.float32
BF16 = jnp.bfloat16


def nn(left, right):
    return lax.dot_general(left, right, (((1,), (0,)), ((), ())), preferred_element_type=F32)


def nt(left, right):
    return lax.dot_general(left, right, (((1,), (1,)), ((), ())), preferred_element_type=F32)


def complex_product(dot, left, right):
    left_real, left_imag = left
    right_real, right_imag = right
    real = dot(left_real, right_real) - dot(left_imag, right_imag)
    imag = dot(left_real, right_imag) + dot(left_imag, right_real)
    return real, imag


def rounded(pair):
    return pair[0].astype(BF16), pair[1].astype(BF16)


def split(pair):
    high = rounded(pair)
    low = rounded((pair[0] - high[0].astype(F32), pair[1] - high[1].astype(F32)))
    return high, low


def plus(left, right):
    return left[0] + right[0], left[1] + right[1]


def couple(rows_h, rows_s, shift_real, shift_imag):
    margin = rows_s.astype(F32)
    real = rows_h.astype(F32) - shift_real * margin
    return real.astype(BF16), (-shift_imag * margin).astype(BF16)


def pivot_inverse(pivot_h, pivot_s, shift_real, shift_imag):
    size = pivot_h.shape[0]
    margin = pivot_s.astype(F32)
    real = pivot_h.astype(F32) - shift_real * margin
    imag = -shift_imag * margin
    on_diagonal = lax.broadcasted_iota(jnp.int32, (size, size), 0) == lax.broadcasted_iota(
        jnp.int32, (size, size), 1
    )
    only_real = jnp.where(on_diagonal, real, 0.0)
    only_imag = jnp.where(on_diagonal, imag, 0.0)

    def start(axis):
        diag_real = jnp.sum(only_real, axis=axis, keepdims=True)
        diag_imag = jnp.sum(only_imag, axis=axis, keepdims=True)
        denom = diag_real * diag_real + diag_imag * diag_imag
        return diag_real / denom, -diag_imag / denom

    left_real, left_imag = start(1)
    right_real, right_imag = start(0)
    identity = jnp.where(on_diagonal, 1.0, 0.0)
    first = (
        identity - (left_real * real - left_imag * imag),
        -(left_real * imag + left_imag * real),
    )
    first_b = rounded(first)
    second = complex_product(nn, first_b, first_b)
    second_b = rounded(second)
    third = complex_product(nn, second_b, first_b)
    fourth_b = rounded(complex_product(nn, second_b, second_b))
    total = plus(plus((identity + first[0], first[1]), second), third)
    total = plus(total, complex_product(nn, rounded(total), fourth_b))
    eighth_b = rounded(complex_product(nn, fourth_b, fourth_b))
    total = plus(total, complex_product(nn, rounded(total), eighth_b))
    return (
        total[0] * right_real - total[1] * right_imag,
        total[0] * right_imag + total[1] * right_real,
    )


def step(
    rows,
    cols,
    poles,
    shift,
    weight,
    pattern,
    front_h,
    front_s,
    panel_h,
    panel_s,
    pivot_h,
    pivot_s,
    ancestor,
    schur_out,
    rows_out,
    pivot_out,
    piv_v,
    own_panel,
    far_panel,
    far_front,
    anc_v,
    schur_v,
    part_rows,
    part_piv,
    send_rows,
    send_piv,
    recv_rows,
    recv_piv,
    layer_send,
    layer_recv,
    final_piv,
    final_rows,
    local_sem,
    panel_ssem,
    panel_rsem,
    front_ssem,
    front_rsem,
    rows_ssem,
    rows_rsem,
    piv_ssem,
    piv_rsem,
    layer_ssem,
    layer_rsem,
    last_ssem,
    last_rsem,
    out_sem,
):
    row = lax.axis_index("row")
    col = lax.axis_index("col")
    pole = lax.axis_index("pole")
    layer = poles * cols
    me = pole * cols + col
    width = front_h.shape[0]
    block = panel_h.shape[0]
    size = pivot_h.shape[0]
    piece = size // poles
    strip = size // cols

    def row_peer(offset):
        return lax.rem(row + offset, rows)

    def layer_peer(offset):
        index = lax.rem(me + offset, layer)
        return index, {"pole": index // cols, "col": lax.rem(index, cols)}

    barrier = pltpu.get_barrier_semaphore()
    for offset in range(1, rows):
        pl.semaphore_signal(
            barrier, inc=1, device_id={"row": row_peer(offset)}, device_id_type=MESH
        )
    for offset in range(1, layer):
        pl.semaphore_signal(
            barrier, inc=1, device_id=layer_peer(offset)[1], device_id_type=MESH
        )

    here = pl.ds(pl.multiple_of(col * width, width), width)
    mine = pl.ds(pl.multiple_of(row * block, block), block)
    local = [
        pltpu.make_async_copy(source, target, local_sem.at[index])
        for index, (source, target) in enumerate(
            [
                (pivot_h, piv_v.at[0]),
                (pivot_s, piv_v.at[1]),
                (panel_h, own_panel.at[0]),
                (panel_s, own_panel.at[1]),
                (ancestor, anc_v),
                (panel_h.at[here, :], far_panel.at[0, row]),
                (panel_s.at[here, :], far_panel.at[1, row]),
                (front_h.at[:, mine], far_front.at[0, row]),
                (front_s.at[:, mine], far_front.at[1, row]),
            ]
        )
    ]
    for copy in local:
        copy.start()
    pl.semaphore_wait(barrier, rows - 1 + layer - 1)

    panel_sends = []
    panel_recvs = []
    front_sends = []
    front_recvs = []
    for offset in range(1, rows):
        to = row_peer(offset)
        origin = lax.rem(row + rows - offset, rows)
        for part, source in enumerate((panel_h, panel_s)):
            panel_sends.append(
                pltpu.make_async_remote_copy(
                    src_ref=source.at[here, :],
                    dst_ref=far_panel.at[part, row],
                    send_sem=panel_ssem.at[part, offset - 1],
                    recv_sem=panel_rsem.at[part, offset - 1],
                    device_id={"row": to},
                    device_id_type=MESH,
                )
            )
            panel_recvs.append(
                pltpu.make_async_remote_copy(
                    src_ref=source.at[here, :],
                    dst_ref=far_panel.at[part, origin],
                    send_sem=panel_ssem.at[part, offset - 1],
                    recv_sem=panel_rsem.at[part, offset - 1],
                    device_id={"row": to},
                    device_id_type=MESH,
                )
            )
        theirs = pl.ds(pl.multiple_of(to * block, block), block)
        for part, source in enumerate((front_h, front_s)):
            front_sends.append(
                pltpu.make_async_remote_copy(
                    src_ref=source.at[:, theirs],
                    dst_ref=far_front.at[part, row],
                    send_sem=front_ssem.at[part, offset - 1],
                    recv_sem=front_rsem.at[part, offset - 1],
                    device_id={"row": to},
                    device_id_type=MESH,
                )
            )
            front_recvs.append(
                pltpu.make_async_remote_copy(
                    src_ref=source.at[:, theirs],
                    dst_ref=far_front.at[part, origin],
                    send_sem=front_ssem.at[part, offset - 1],
                    recv_sem=front_rsem.at[part, offset - 1],
                    device_id={"row": to},
                    device_id_type=MESH,
                )
            )
    for copy in panel_sends + front_sends:
        copy.start()

    shift_real = shift[0, 0]
    shift_imag = shift[0, 1]
    weight_real = weight[0, 0]
    weight_imag = weight[0, 1]

    local[0].wait()
    local[1].wait()
    inverse = pivot_inverse(piv_v[0], piv_v[1], shift_real, shift_imag)
    inv_high, inv_low = split(inverse)
    for copy in local[2:]:
        copy.wait()
    coupling = couple(own_panel[0], own_panel[1], shift_real, shift_imag)
    flipped = rounded(
        plus(
            complex_product(nt, inv_high, coupling),
            complex_product(nt, inv_low, coupling),
        )
    )
    anc = (
        anc_v[0].reshape(rows * width, block).T,
        anc_v[1].reshape(rows * width, block).T,
    )

    for copy in panel_recvs:
        copy.wait_recv()
    far_coupling = couple(
        far_panel[0].reshape(rows * width, size),
        far_panel[1].reshape(rows * width, size),
        shift_real,
        shift_imag,
    )
    solved = rounded(
        plus(
            complex_product(nn, far_coupling, inv_high),
            complex_product(nn, far_coupling, inv_low),
        )
    )
    part = complex_product(nn, anc, solved)
    weighted_imag = -(weight_real * part[1] + weight_imag * part[0])
    weighted_real = -(weight_real * part[0] - weight_imag * part[1])

    def scatter(value, kept, sent, height):
        for index in range(layer):
            tile = value[
                (index % cols) * height : (index % cols + 1) * height,
                (index // cols) * piece : (index // cols + 1) * piece,
            ]
            kept[index] = tile
            sent[index] = tile.astype(BF16)

    def exchange(sent, received, ssem, rsem):
        copies = []
        for offset in range(1, layer):
            index, device = layer_peer(offset)
            copies.append(
                pltpu.make_async_remote_copy(
                    src_ref=sent.at[index],
                    dst_ref=received.at[offset - 1],
                    send_sem=ssem.at[offset - 1],
                    recv_sem=rsem.at[offset - 1],
                    device_id=device,
                    device_id_type=MESH,
                )
            )
        for copy in copies:
            copy.start()
        return copies

    corr = nn(flipped[0], weighted_imag.astype(BF16)) + nn(
        flipped[1], weighted_real.astype(BF16)
    )
    share = (weight_real * inverse[1] + weight_imag * inverse[0]) * (1.0 / (rows * cols)) - corr
    scatter(share, part_piv, send_piv, strip)
    piv_copies = exchange(send_piv, recv_piv, piv_ssem, piv_rsem)
    scatter(weighted_imag, part_rows, send_rows, width)
    rows_copies = exchange(send_rows, recv_rows, rows_ssem, rows_rsem)

    update = complex_product(nt, solved, coupling)

    for copy in piv_copies:
        copy.wait_recv()
    layer_sum = part_piv[me]
    for offset in range(layer - 1):
        layer_sum = layer_sum + recv_piv[offset].astype(F32)
    layer_send[...] = layer_sum
    layer_copies = [
        pltpu.make_async_remote_copy(
            src_ref=layer_send,
            dst_ref=layer_recv.at[offset - 1],
            send_sem=layer_ssem.at[offset - 1],
            recv_sem=layer_rsem.at[offset - 1],
            device_id={"row": row_peer(offset)},
            device_id_type=MESH,
        )
        for offset in range(1, rows)
    ]
    for copy in layer_copies:
        copy.start()

    for copy in front_recvs:
        copy.wait_recv()
    for index in range(rows):
        flag = pattern[index, row].astype(F32)
        margin = far_front[1, index].astype(F32)
        hamil = far_front[0, index].astype(F32)
        at = slice(index * width, (index + 1) * width)
        schur_v[0, index] = (flag * (hamil - shift_real * margin) - update[0][at]).astype(BF16)
        schur_v[1, index] = (flag * (-shift_imag * margin) - update[1][at]).astype(BF16)
    schur_copy = pltpu.make_async_copy(schur_v, schur_out, out_sem.at[0])
    schur_copy.start()

    for copy in layer_copies:
        copy.wait_recv()
    whole = layer_sum
    for offset in range(rows - 1):
        whole = whole + layer_recv[offset]
    final_piv[col] = whole
    last_copies = []
    last_recvs = []
    for offset in range(1, cols):
        to = lax.rem(col + offset, cols)
        origin = lax.rem(col + cols - offset, cols)
        for slot, group in ((col, last_copies), (origin, last_recvs)):
            group.append(
                pltpu.make_async_remote_copy(
                    src_ref=final_piv.at[col],
                    dst_ref=final_piv.at[slot],
                    send_sem=last_ssem.at[offset - 1],
                    recv_sem=last_rsem.at[offset - 1],
                    device_id={"col": to},
                    device_id_type=MESH,
                )
            )
    for copy in last_copies:
        copy.start()

    for copy in rows_copies:
        copy.wait_recv()
    rows_sum = part_rows[me]
    for offset in range(layer - 1):
        rows_sum = rows_sum + recv_rows[offset].astype(F32)
    final_rows[...] = rows_sum
    rows_copy = pltpu.make_async_copy(final_rows, rows_out, out_sem.at[1])
    rows_copy.start()

    for copy in last_recvs:
        copy.wait_recv()
    pivot_copy = pltpu.make_async_copy(final_piv, pivot_out, out_sem.at[2])
    pivot_copy.start()
    for copy in panel_sends + front_sends + piv_copies + rows_copies:
        copy.wait_send()
    for copy in layer_copies + last_copies:
        copy.wait_send()
    schur_copy.wait()
    rows_copy.wait()
    pivot_copy.wait()


def shards(
    rows,
    cols,
    poles,
    front_h,
    front_s,
    panel_h,
    panel_s,
    pivot_h,
    pivot_s,
    pole_shift,
    pole_weight,
    pattern,
    ancestor_inverse,
):
    width = front_h.shape[0]
    block = panel_h.shape[0]
    size = pivot_h.shape[0]
    piece = size // poles
    strip = size // cols
    layer = poles * cols
    ancestor = ancestor_inverse.reshape(2, rows, width, block)
    smem = pl.BlockSpec(memory_space=pltpu.SMEM)
    anywhere = pl.BlockSpec(memory_space=pl.ANY)
    dma = pltpu.SemaphoreType.DMA
    schur, rows_out, pivot_out = pl.pallas_call(
        functools.partial(step, rows, cols, poles),
        out_shape=(
            jax.ShapeDtypeStruct((2, rows, width, block), BF16),
            jax.ShapeDtypeStruct((width, piece), F32),
            jax.ShapeDtypeStruct((cols, strip, piece), F32),
        ),
        in_specs=[smem] * 3 + [anywhere] * 7,
        out_specs=(anywhere,) * 3,
        scratch_shapes=[
            pltpu.VMEM((2, size, size), BF16),
            pltpu.VMEM((2, block, size), BF16),
            pltpu.VMEM((2, rows, width, size), BF16),
            pltpu.VMEM((2, rows, width, block), BF16),
            pltpu.VMEM((2, rows, width, block), BF16),
            pltpu.VMEM((2, rows, width, block), BF16),
            pltpu.VMEM((layer, width, piece), F32),
            pltpu.VMEM((layer, strip, piece), F32),
            pltpu.VMEM((layer, width, piece), BF16),
            pltpu.VMEM((layer, strip, piece), BF16),
            pltpu.VMEM((layer - 1, width, piece), BF16),
            pltpu.VMEM((layer - 1, strip, piece), BF16),
            pltpu.VMEM((strip, piece), F32),
            pltpu.VMEM((rows - 1, strip, piece), F32),
            pltpu.VMEM((cols, strip, piece), F32),
            pltpu.VMEM((width, piece), F32),
            dma((9,)),
            dma((2, rows - 1)),
            dma((2, rows - 1)),
            dma((2, rows - 1)),
            dma((2, rows - 1)),
            dma((layer - 1,)),
            dma((layer - 1,)),
            dma((layer - 1,)),
            dma((layer - 1,)),
            dma((rows - 1,)),
            dma((rows - 1,)),
            dma((cols - 1,)),
            dma((cols - 1,)),
            dma((3,)),
        ],
        compiler_params=pltpu.CompilerParams(
            collective_id=0, has_side_effects=True, vmem_limit_bytes=48 * 1024 * 1024
        ),
        name="front_step",
    )(
        pole_shift,
        pole_weight,
        pattern,
        front_h,
        front_s,
        panel_h,
        panel_s,
        pivot_h,
        pivot_s,
        ancestor,
    )
    return (
        schur.reshape(ancestor_inverse.shape),
        rows_out,
        pivot_out.reshape(size, piece),
    )


def solution(mesh):
    sizes = dict(mesh.shape)
    in_specs = (
        P(("row", "col"), None),
        P(("row", "col"), None),
        P("row", None),
        P("row", None),
        P(),
        P(),
        P("pole", None),
        P("pole", None),
        P(),
        P("pole", None, None, "col", None, "row"),
    )
    out_specs = (
        P("pole", None, None, "col", None, "row"),
        P(("row", "col"), "pole"),
        P(None, "pole"),
    )
    body = functools.partial(shards, sizes["row"], sizes["col"], sizes["pole"])
    return jax.shard_map(body, mesh=mesh, in_specs=in_specs, out_specs=out_specs, check_vma=False)
```

time: 218 us -> 40.4 us (0.19)
  waiting for transfers between devices: 127 us -> 0 us
  Pallas kernels: 0 us -> 29.7 us
  matrix products: 20.5 us -> 0 us
  blocking collectives: 15.8 us -> 0 us
  between operations: 15.4 us -> 0.67 us
  starting transfers between devices: 10.3 us -> 0 us
  other arithmetic: 9.35 us -> 0 us
  local copies, waits for them, and re-layouts: 18.6 us -> 9.68 us
    psum x2 -> x0, waiting for transfers between devices: 112 us -> none  [the longest x1 88.1 us: shards(): correction = lax.psum(jnp.stack([corr_real, corr_imag]), ('row', 'col'))]
    pallas_call x0 -> x1, Pallas kernels: none -> 29.7 us  [shards(): pl.pallas_call(functools.partial(step, rows, cols, poles), out_shape=(jax...]
    dot_general x48 -> x0, matrix products: 20.5 us -> none  [the longest x9 4.36 us: complex_matmul(): jnp.dot(left_imag, right_real, precision=highest, preferred_element_type=...]
    all_gather x1 -> x0, blocking collectives: 15.8 us -> none  [shards(): far_solved = lax.all_gather(solved_strip, 'row', axis=1, tiled=True)]
    all_to_all x2 -> x0, starting transfers between devices: 10.3 us -> none  [the longest x1 5.16 us: shards(): lax.all_to_all(front_h, 'row', split_axis=1, concat_axis=0, tiled=True)]
    unnamed x4 -> x0, waiting for transfers between devices: 9.15 us -> none
    gather x5 -> x0, local copies, waits for them, and re-layouts: 6.52 us -> none  [the longest x1 2.34 us: invert_pivot(): diag_real = jnp.diagonal(matrix_real)]
    all_to_all x2 -> x0, waiting for transfers between devices: 5.7 us -> none  [the longest x1 5.7 us: shards(): lax.all_to_all(front_s, 'row', split_axis=1, concat_axis=0, tiled=True)]
  transfers between devices with their start and end apart: 5 -> 0, of which waited for: 4 -> 0; matrix products, arithmetic and copies ran while one was open for 4% -> 0% of each run, Pallas kernels for 0% -> 0%
where the time goes in v1:
time: 40.4 us; the launch traced here: 40.1 us
  Pallas kernels  29.7 us (74%)
  local copies, waits for them, and re-layouts  9.68 us (24%)
  between operations  0.67 us (2%)
    pallas_call x1, Pallas kernels, shards(): pl.pallas_call(functools.partial(step, rows, cols, poles), out_shape=(jax...  29.7 us
    unnamed x23, local copies, waits for them, and re-layouts  9.68 us

profile of v1, /device:TPU:0, one launch (start us, length us, event | category | flops | bytes accessed | tf_op | source)
XLA Modules:
  0.0 40.1 jit_solution(11371199109388304613)
XLA Ops:
  0.6 0.0 copy-start.9
  0.6 0.0 copy-start.8
  0.7 0.6 %copy-done.9 = f32[1,2]{1,0:T(1,128)S(1)} copy-done((f32[1,2]{1,0:T(1,128)S(1)}, f32[1,2]{1,0:T(1,128)}, u32[]{:S(2)}) %copy-start.9) | copy-done | bytes 32
  1.3 0.0 copy-done.8
  1.3 0.0 copy-start
  1.3 0.9 %copy-done = bf16[1,2,4,1,64,256]{5,4,3,2,1,0:T(8,128)(2,1)S(1)} copy-done((bf16[1,2,4,1,64,256]{5,4,3,2,1,0:T(8,128)(2,1)S(1)}, bf16[1,2,4,1,64,256]{5,4,3,2,1,0:T(8,128)(2,1)}, u32[]{:S(2)}) %copy-start) | copy-done | bytes 262168
  2.3 0.0 copy-start.1
  2.3 0.9 %copy-done.1 = bf16[64,1024]{1,0:T(8,128)(2,1)S(1)} copy-done((bf16[64,1024]{1,0:T(8,128)(2,1)S(1)}, bf16[64,1024]{1,0:T(8,128)(2,1)}, u32[]{:S(2)}) %copy-start.1) | copy-done | bytes 131096
  3.2 0.0 copy-start.2
  3.2 0.9 %copy-done.2 = bf16[64,1024]{1,0:T(8,128)(2,1)S(1)} copy-done((bf16[64,1024]{1,0:T(8,128)(2,1)S(1)}, bf16[64,1024]{1,0:T(8,128)(2,1)}, u32[]{:S(2)}) %copy-start.2) | copy-done | bytes 131096
  4.1 0.0 copy-start.3
  4.1 0.9 %copy-done.3 = bf16[256,256]{1,0:T(8,128)(2,1)S(1)} copy-done((bf16[256,256]{1,0:T(8,128)(2,1)S(1)}, bf16[256,256]{1,0:T(8,128)(2,1)}, u32[]{:S(2)}) %copy-start.3) | copy-done | bytes 131096
  5.0 0.0 copy-start.4
  5.0 0.9 %copy-done.4 = bf16[256,256]{1,0:T(8,128)(2,1)S(1)} copy-done((bf16[256,256]{1,0:T(8,128)(2,1)S(1)}, bf16[256,256]{1,0:T(8,128)(2,1)}, u32[]{:S(2)}) %copy-start.4) | copy-done | bytes 131096
  5.9 0.0 copy-start.5
  5.9 0.9 %copy-done.5 = bf16[256,256]{1,0:T(8,128)(2,1)S(1)} copy-done((bf16[256,256]{1,0:T(8,128)(2,1)S(1)}, bf16[256,256]{1,0:T(8,128)(2,1)}, u32[]{:S(2)}) %copy-start.5) | copy-done | bytes 131096
  6.8 0.0 copy-start.6
  6.8 0.9 %copy-done.6 = bf16[256,256]{1,0:T(8,128)(2,1)S(1)} copy-done((bf16[256,256]{1,0:T(8,128)(2,1)S(1)}, bf16[256,256]{1,0:T(8,128)(2,1)}, u32[]{:S(2)}) %copy-start.6) | copy-done | bytes 131096
  7.7 0.0 copy-start.7
  7.7 0.7 %copy-done.7 = s32[4,4]{1,0:T(4,128)S(1)} copy-done((s32[4,4]{1,0:T(4,128)S(1)}, s32[4,4]{1,0:T(4,128)}, u32[]{:S(2)}) %copy-start.7) | copy-done | bytes 88
  8.4 29.7 %front_step.1 = (bf16[2,4,64,256]{3,2,1,0:T(8,128)(2,1)S(1)}, f32[64,128]{1,0:T(8,128)S(1)}, f32[4,64,128]{2,1,0:T(8,128)S(1)}) custom-call(f32[1,2]{1,0:T(1,128)S(1)} %copy-done.8, f32[1,2]{1,0:T(1,128)S(1)} %copy-done.9, s32[4,4]{1,0:T(4,128)S(1)} %copy-done.7, bf16[64,1024]{1,0:T(8,128)(2,1)S(1)} %copy-done.1, bf16[64,1024]{1,0:T(8,128)(2,1)S(1)} %copy-done.2, ...), custom_call_target="tpu_custom_call" | custom-call | tf_op jit(solution)/shard_map/front_step/pallas_call | solution.py:424
  38.1 0.7 %copy.17 = bf16[1,2,4,1,64,256]{5,4,3,2,1,0:T(8,128)(2,1)} copy(bf16[1,2,4,1,64,256]{5,4,3,2,1,0:T(8,128)(2,1)S(1)} %bitcast.6) | data formatting | bytes 524288
  38.8 0.6 %copy.18 = f32[64,128]{1,0:T(8,128)} copy(f32[64,128]{1,0:T(8,128)S(1)} %get-tuple-element.16) | data formatting | bytes 65536
  39.4 0.7 %copy.19 = f32[256,128]{1,0:T(8,128)} copy(f32[256,128]{1,0:T(8,128)S(1)} %bitcast.7) | data formatting | bytes 262144
Async XLA Ops:
  0.6 0.7 %copy-start.9 = (f32[1,2]{1,0:T(1,128)S(1)}, f32[1,2]{1,0:T(1,128)}, u32[]{:S(2)}) copy-start(f32[1,2]{1,0:T(1,128)} %weight.1) | copy-start | bytes 28
  0.6 0.7 %copy-start.8 = (f32[1,2]{1,0:T(1,128)S(1)}, f32[1,2]{1,0:T(1,128)}, u32[]{:S(2)}) copy-start(f32[1,2]{1,0:T(1,128)} %shift.1) | copy-start | bytes 28
  1.3 0.9 %copy-start = (bf16[1,2,4,1,64,256]{5,4,3,2,1,0:T(8,128)(2,1)S(1)}, bf16[1,2,4,1,64,256]{5,4,3,2,1,0:T(8,128)(2,1)}, u32[]{:S(2)}) copy-start(bf16[1,2,4,1,64,256]{5,4,3,2,1,0:T(8,128)(2,1)} %param.19) | copy-start | bytes 786436
  2.3 0.9 %copy-start.1 = (bf16[64,1024]{1,0:T(8,128)(2,1)S(1)}, bf16[64,1024]{1,0:T(8,128)(2,1)}, u32[]{:S(2)}) copy-start(bf16[64,1024]{1,0:T(8,128)(2,1)} %front_h.1) | copy-start | bytes 393220
  3.2 0.9 %copy-start.2 = (bf16[64,1024]{1,0:T(8,128)(2,1)S(1)}, bf16[64,1024]{1,0:T(8,128)(2,1)}, u32[]{:S(2)}) copy-start(bf16[64,1024]{1,0:T(8,128)(2,1)} %front_s.1) | copy-start | bytes 393220
  4.1 0.9 %copy-start.3 = (bf16[256,256]{1,0:T(8,128)(2,1)S(1)}, bf16[256,256]{1,0:T(8,128)(2,1)}, u32[]{:S(2)}) copy-start(bf16[256,256]{1,0:T(8,128)(2,1)} %panel_h.1) | copy-start | bytes 393220
  5.0 0.9 %copy-start.4 = (bf16[256,256]{1,0:T(8,128)(2,1)S(1)}, bf16[256,256]{1,0:T(8,128)(2,1)}, u32[]{:S(2)}) copy-start(bf16[256,256]{1,0:T(8,128)(2,1)} %panel_s.1) | copy-start | bytes 393220
  5.9 0.9 %copy-start.5 = (bf16[256,256]{1,0:T(8,128)(2,1)S(1)}, bf16[256,256]{1,0:T(8,128)(2,1)}, u32[]{:S(2)}) copy-start(bf16[256,256]{1,0:T(8,128)(2,1)} %pivot_h.1) | copy-start | bytes 393220
  6.8 0.9 %copy-start.6 = (bf16[256,256]{1,0:T(8,128)(2,1)S(1)}, bf16[256,256]{1,0:T(8,128)(2,1)}, u32[]{:S(2)}) copy-start(bf16[256,256]{1,0:T(8,128)(2,1)} %pivot_s.1) | copy-start | bytes 393220
  7.7 0.7 %copy-start.7 = (s32[4,4]{1,0:T(4,128)S(1)}, s32[4,4]{1,0:T(4,128)}, u32[]{:S(2)}) copy-start(s32[4,4]{1,0:T(4,128)} %pattern.1) | copy-start | bytes 196

commit v2 on v1

--- a/solution.py
+++ b/solution.py
@@ -20,12 +20,31 @@
     return lax.dot_general(left, right, (((1,), (1,)), ((), ())), preferred_element_type=F32)
 
 
-def complex_product(dot, left, right):
-    left_real, left_imag = left
-    right_real, right_imag = right
-    real = dot(left_real, right_real) - dot(left_imag, right_imag)
-    imag = dot(left_real, right_imag) + dot(left_imag, right_real)
-    return real, imag
+def side(pair):
+    return jnp.concatenate(pair, axis=1)
+
+
+def below(pair):
+    real, imag = pair
+    return jnp.concatenate([side((real, imag)), side((-imag, real))], axis=0)
+
+
+def across(pair):
+    real, imag = pair
+    return jnp.concatenate([side((real, -imag)), side((imag, real))], axis=0)
+
+
+def halves(value):
+    middle = value.shape[1] // 2
+    return value[:, :middle], value[:, middle:]
+
+
+def product(left, right):
+    return halves(nn(side(left), below(right)))
+
+
+def product_nt(left, right):
+    return halves(nt(side(left), across(right)))
 
 
 def rounded(pair):
@@ -73,14 +92,19 @@
         -(left_real * imag + left_imag * real),
     )
     first_b = rounded(first)
-    second = complex_product(nn, first_b, first_b)
+    first_below = below(first_b)
+    second = halves(nn(side(first_b), first_below))
     second_b = rounded(second)
-    third = complex_product(nn, second_b, first_b)
-    fourth_b = rounded(complex_product(nn, second_b, second_b))
+    wide = nn(side(second_b), jnp.concatenate([first_below, below(second_b)], axis=1))
+    third = halves(wide[:, : 2 * size])
+    fourth_b = rounded(halves(wide[:, 2 * size :]))
     total = plus(plus((identity + first[0], first[1]), second), third)
-    total = plus(total, complex_product(nn, rounded(total), fourth_b))
-    eighth_b = rounded(complex_product(nn, fourth_b, fourth_b))
-    total = plus(total, complex_product(nn, rounded(total), eighth_b))
+    tall = nn(
+        jnp.concatenate([side(fourth_b), side(rounded(total))], axis=0), below(fourth_b)
+    )
+    eighth_b = rounded(halves(tall[:size]))
+    total = plus(total, halves(tall[size:]))
+    total = plus(total, product(rounded(total), eighth_b))
     return (
         total[0] * right_real - total[1] * right_imag,
         total[0] * right_imag + total[1] * right_real,
@@ -91,9 +115,9 @@
     rows,
     cols,
     poles,
-    shift,
-    weight,
-    pattern,
+    shift_hbm,
+    weight_hbm,
+    pattern_hbm,
     front_h,
     front_s,
     panel_h,
@@ -104,12 +128,17 @@
     schur_out,
     rows_out,
     pivot_out,
+    shift,
+    weight,
+    pattern,
     piv_v,
     own_panel,
     far_panel,
     far_front,
     anc_v,
     schur_v,
+    final_rows,
+    final_piv,
     part_rows,
     part_piv,
     send_rows,
@@ -118,8 +147,6 @@
     recv_piv,
     layer_send,
     layer_recv,
-    final_piv,
-    final_rows,
     local_sem,
     panel_ssem,
     panel_rsem,
@@ -169,8 +196,11 @@
         pltpu.make_async_copy(source, target, local_sem.at[index])
         for index, (source, target) in enumerate(
             [
+                (shift_hbm, shift),
                 (pivot_h, piv_v.at[0]),
                 (pivot_s, piv_v.at[1]),
+                (weight_hbm, weight),
+                (pattern_hbm, pattern),
                 (panel_h, own_panel.at[0]),
                 (panel_s, own_panel.at[1]),
                 (ancestor, anc_v),
@@ -235,49 +265,56 @@
                     device_id_type=MESH,
                 )
             )
-    for copy in panel_sends + front_sends:
+    for copy in panel_sends:
         copy.start()
 
+    for copy in local[:3]:
+        copy.wait()
     shift_real = shift[0, 0]
     shift_imag = shift[0, 1]
+    inverse = pivot_inverse(piv_v[0], piv_v[1], shift_real, shift_imag)
+    inv_high, inv_low = split(inverse)
+    for copy in local[3:]:
+        copy.wait()
     weight_real = weight[0, 0]
     weight_imag = weight[0, 1]
-
-    local[0].wait()
-    local[1].wait()
-    inverse = pivot_inverse(piv_v[0], piv_v[1], shift_real, shift_imag)
-    inv_high, inv_low = split(inverse)
-    for copy in local[2:]:
-        copy.wait()
     coupling = couple(own_panel[0], own_panel[1], shift_real, shift_imag)
+    coupling_across = across(coupling)
     flipped = rounded(
-        plus(
-            complex_product(nt, inv_high, coupling),
-            complex_product(nt, inv_low, coupling),
+        halves(nt(side(inv_high), coupling_across) + nt(side(inv_low), coupling_across))
+    )
+    anc = (
+        anc_v[0].reshape(rows * width, block),
+        anc_v[1].reshape(rows * width, block),
+    )
+    swept = product_nt(flipped, anc)
+    swept_both = side(
+        rounded(
+            (
+                weight_real * swept[1] + weight_imag * swept[0],
+                weight_real * swept[0] - weight_imag * swept[1],
+            )
         )
     )
-    anc = (
-        anc_v[0].reshape(rows * width, block).T,
-        anc_v[1].reshape(rows * width, block).T,
-    )
-
+    own_share = (weight_real * inverse[1] + weight_imag * inverse[0]) * (1.0 / (rows * cols))
+    anc_flipped = side((anc[0].T, anc[1].T))
+    inv_below = jnp.concatenate([below(inv_high), below(inv_low)], axis=0)
+
+    for copy in panel_sends:
+        copy.wait_send()
+    for copy in front_sends:
+        copy.start()
     for copy in panel_recvs:
         copy.wait_recv()
-    far_coupling = couple(
-        far_panel[0].reshape(rows * width, size),
-        far_panel[1].reshape(rows * width, size),
-        shift_real,
-        shift_imag,
-    )
-    solved = rounded(
-        plus(
-            complex_product(nn, far_coupling, inv_high),
-            complex_product(nn, far_coupling, inv_low),
+    far_coupling = side(
+        couple(
+            far_panel[0].reshape(rows * width, size),
+            far_panel[1].reshape(rows * width, size),
+            shift_real,
+            shift_imag,
         )
     )
-    part = complex_product(nn, anc, solved)
-    weighted_imag = -(weight_real * part[1] + weight_imag * part[0])
-    weighted_real = -(weight_real * part[0] - weight_imag * part[1])
+    solved = rounded(halves(nn(jnp.concatenate([far_coupling, far_coupling], axis=1), inv_below)))
 
     def scatter(value, kept, sent, height):
         for index in range(layer):
@@ -306,23 +343,22 @@
             copy.start()
         return copies
 
-    corr = nn(flipped[0], weighted_imag.astype(BF16)) + nn(
-        flipped[1], weighted_real.astype(BF16)
-    )
-    share = (weight_real * inverse[1] + weight_imag * inverse[0]) * (1.0 / (rows * cols)) - corr
+    share = own_share + nn(swept_both, jnp.concatenate(solved, axis=0))
     scatter(share, part_piv, send_piv, strip)
     piv_copies = exchange(send_piv, recv_piv, piv_ssem, piv_rsem)
+    part = halves(nn(anc_flipped, below(solved)))
+    weighted_imag = -(weight_real * part[1] + weight_imag * part[0])
     scatter(weighted_imag, part_rows, send_rows, width)
     rows_copies = exchange(send_rows, recv_rows, rows_ssem, rows_rsem)
 
-    update = complex_product(nt, solved, coupling)
+    update = halves(nt(side(solved), coupling_across))
 
     for copy in piv_copies:
         copy.wait_recv()
     layer_sum = part_piv[me]
     for offset in range(layer - 1):
         layer_sum = layer_sum + recv_piv[offset].astype(F32)
-    layer_send[...] = layer_sum
+    layer_send[...] = layer_sum.astype(BF16)
     layer_copies = [
         pltpu.make_async_remote_copy(
             src_ref=layer_send,
@@ -346,6 +382,7 @@
         at = slice(index * width, (index + 1) * width)
         schur_v[0, index] = (flag * (hamil - shift_real * margin) - update[0][at]).astype(BF16)
         schur_v[1, index] = (flag * (-shift_imag * margin) - update[1][at]).astype(BF16)
+
     schur_copy = pltpu.make_async_copy(schur_v, schur_out, out_sem.at[0])
     schur_copy.start()
 
@@ -353,8 +390,10 @@
         copy.wait_recv()
     whole = layer_sum
     for offset in range(rows - 1):
-        whole = whole + layer_recv[offset]
-    final_piv[col] = whole
+        whole = whole + layer_recv[offset].astype(F32)
+    final_piv[...] = whole
+    own_copy = pltpu.make_async_copy(final_piv, pivot_out.at[col], out_sem.at[2])
+    own_copy.start()
     last_copies = []
     last_recvs = []
     for offset in range(1, cols):
@@ -363,8 +402,8 @@
         for slot, group in ((col, last_copies), (origin, last_recvs)):
             group.append(
                 pltpu.make_async_remote_copy(
-                    src_ref=final_piv.at[col],
-                    dst_ref=final_piv.at[slot],
+                    src_ref=final_piv,
+                    dst_ref=pivot_out.at[slot],
                     send_sem=last_ssem.at[offset - 1],
                     recv_sem=last_rsem.at[offset - 1],
                     device_id={"col": to},
@@ -385,15 +424,25 @@
 
     for copy in last_recvs:
         copy.wait_recv()
-    pivot_copy = pltpu.make_async_copy(final_piv, pivot_out, out_sem.at[2])
-    pivot_copy.start()
-    for copy in panel_sends + front_sends + piv_copies + rows_copies:
+    for copy in front_sends + piv_copies + rows_copies:
         copy.wait_send()
     for copy in layer_copies + last_copies:
         copy.wait_send()
     schur_copy.wait()
     rows_copy.wait()
-    pivot_copy.wait()
+    own_copy.wait()
+
+
+def hand_over(*refs):
+    sources, targets, sem = refs[:3], refs[3:6], refs[6]
+    copies = [
+        pltpu.make_async_copy(source, target, sem.at[index])
+        for index, (source, target) in enumerate(zip(sources, targets))
+    ]
+    for copy in copies:
+        copy.start()
+    for copy in copies:
+        copy.wait()
 
 
 def shards(
@@ -418,36 +467,39 @@
     strip = size // cols
     layer = poles * cols
     ancestor = ancestor_inverse.reshape(2, rows, width, block)
-    smem = pl.BlockSpec(memory_space=pltpu.SMEM)
-    anywhere = pl.BlockSpec(memory_space=pl.ANY)
+    hbm = pl.BlockSpec(memory_space=pl.ANY)
     dma = pltpu.SemaphoreType.DMA
-    schur, rows_out, pivot_out = pl.pallas_call(
+    out_shape = (
+        jax.ShapeDtypeStruct((2, rows, width, block), BF16),
+        jax.ShapeDtypeStruct((width, piece), F32),
+        jax.ShapeDtypeStruct((cols, strip, piece), F32),
+    )
+    found = pl.pallas_call(
         functools.partial(step, rows, cols, poles),
-        out_shape=(
-            jax.ShapeDtypeStruct((2, rows, width, block), BF16),
-            jax.ShapeDtypeStruct((width, piece), F32),
-            jax.ShapeDtypeStruct((cols, strip, piece), F32),
-        ),
-        in_specs=[smem] * 3 + [anywhere] * 7,
-        out_specs=(anywhere,) * 3,
+        out_shape=out_shape,
+        in_specs=[hbm] * 10,
+        out_specs=(hbm,) * 3,
         scratch_shapes=[
+            pltpu.SMEM(pole_shift.shape, F32),
+            pltpu.SMEM(pole_weight.shape, F32),
+            pltpu.SMEM(pattern.shape, jnp.int32),
             pltpu.VMEM((2, size, size), BF16),
             pltpu.VMEM((2, block, size), BF16),
             pltpu.VMEM((2, rows, width, size), BF16),
             pltpu.VMEM((2, rows, width, block), BF16),
             pltpu.VMEM((2, rows, width, block), BF16),
             pltpu.VMEM((2, rows, width, block), BF16),
+            pltpu.VMEM((width, piece), F32),
+            pltpu.VMEM((strip, piece), F32),
             pltpu.VMEM((layer, width, piece), F32),
             pltpu.VMEM((layer, strip, piece), F32),
             pltpu.VMEM((layer, width, piece), BF16),
             pltpu.VMEM((layer, strip, piece), BF16),
             pltpu.VMEM((layer - 1, width, piece), BF16),
             pltpu.VMEM((layer - 1, strip, piece), BF16),
-            pltpu.VMEM((strip, piece), F32),
-            pltpu.VMEM((rows - 1, strip, piece), F32),
-            pltpu.VMEM((cols, strip, piece), F32),
-            pltpu.VMEM((width, piece), F32),
-            dma((9,)),
+            pltpu.VMEM((strip, piece), BF16),
+            pltpu.VMEM((rows - 1, strip, piece), BF16),
+            dma((12,)),
             dma((2, rows - 1)),
             dma((2, rows - 1)),
             dma((2, rows - 1)),
@@ -463,7 +515,7 @@
             dma((3,)),
         ],
         compiler_params=pltpu.CompilerParams(
-            collective_id=0, has_side_effects=True, vmem_limit_bytes=48 * 1024 * 1024
+            collective_id=0, has_side_effects=True, vmem_limit_bytes=60 * 1024 * 1024
         ),
         name="front_step",
     )(
@@ -478,6 +530,15 @@
         pivot_s,
         ancestor,
     )
+    schur, rows_out, pivot_out = pl.pallas_call(
+        hand_over,
+        out_shape=out_shape,
+        in_specs=[hbm] * 3,
+        out_specs=(hbm,) * 3,
+        scratch_shapes=[dma((3,))],
+        compiler_params=pltpu.CompilerParams(vmem_limit_bytes=60 * 1024 * 1024),
+        name="hand_over",
+    )(*found)
     return (
         schur.reshape(ancestor_inverse.shape),
         rows_out,

time: 40.4 us -> 43.1 us (1.067)
  Pallas kernels: 29.7 us -> 42.3 us
  local copies, waits for them, and re-layouts: 9.68 us -> 0 us
    pallas_call x1 -> x2, Pallas kernels: 29.7 us -> 42.3 us  [the longest x1 28.3 us: shards(): pl.pallas_call(functools.partial(step, rows, cols, poles), out_shape=out_...]
    unnamed x23 -> x0, local copies, waits for them, and re-layouts: 9.68 us -> none
where the time goes in v2:
time: 43.1 us; the launch traced here: 43 us
  Pallas kernels  42.3 us (98%)
  between operations  0.64 us (1%)
    pallas_call x1, Pallas kernels, shards(): pl.pallas_call(functools.partial(step, rows, cols, poles), out_shape=out_...  28.3 us
    pallas_call x1, Pallas kernels, shards(): pl.pallas_call(hand_over, out_shape=out_shape, in_specs=[hbm] * 3, out_sp...  14 us

profile of v2, /device:TPU:0, one launch (start us, length us, event | category | flops | bytes accessed | tf_op | source)
XLA Modules:
  0.0 43.0 jit_solution(120655898077909009)
XLA Ops:
  0.6 28.3 %front_step.1 = (bf16[2,4,64,256]{3,2,1,0:T(8,128)(2,1)}, f32[64,128]{1,0:T(8,128)}, f32[4,64,128]{2,1,0:T(8,128)}) custom-call(f32[1,2]{1,0:T(1,128)} %shift_hbm.1, f32[1,2]{1,0:T(1,128)} %weight_hbm.1, s32[4,4]{1,0:T(4,128)} %pattern_hbm.1, bf16[64,1024]{1,0:T(8,128)(2,1)} %front_h.1, bf16[64,1024]{1,0:T(8,128)(2,1)} %front_s.1, bf16[256,256]{1,0:T(8,128)(2,1)} %panel_h.1, ...), custom_call_target="tpu_custom_call" | custom-call | tf_op jit(solution)/shard_map/front_step/pallas_call | solution.py:477
  28.9 14.0 %hand_over.1 = (bf16[2,4,64,256]{3,2,1,0:T(8,128)(2,1)}, f32[64,128]{1,0:T(8,128)}, f32[4,64,128]{2,1,0:T(8,128)}) custom-call(bf16[2,4,64,256]{3,2,1,0:T(8,128)(2,1)} %get-tuple-element.9.refs_0_, f32[64,128]{1,0:T(8,128)} %get-tuple-element.10.refs_1_, f32[4,64,128]{2,1,0:T(8,128)} %get-tuple-element.11.refs_2_), custom_call_target="tpu_custom_call" | custom-call | tf_op jit(solution)/shard_map/hand_over/pallas_call | solution.py:533

commit v3 on v2

--- a/solution.py
+++ b/solution.py
@@ -147,6 +147,8 @@
     recv_piv,
     layer_send,
     layer_recv,
+    pass_ssem,
+    pass_rsem,
     local_sem,
     panel_ssem,
     panel_rsem,
@@ -215,8 +217,15 @@
         copy.start()
     pl.semaphore_wait(barrier, rows - 1 + layer - 1)
 
+    shares = poles if width % (16 * poles) == 0 else 1
+    height = width // shares
+    first = pl.multiple_of(pole * height if shares > 1 else 0, height)
+    held = pl.ds(first, height)
+    source_rows = pl.ds(pl.multiple_of(col * width + first, height), height)
     panel_sends = []
     panel_recvs = []
+    panel_passes = []
+    passed_recvs = []
     front_sends = []
     front_recvs = []
     for offset in range(1, rows):
@@ -225,8 +234,8 @@
         for part, source in enumerate((panel_h, panel_s)):
             panel_sends.append(
                 pltpu.make_async_remote_copy(
-                    src_ref=source.at[here, :],
-                    dst_ref=far_panel.at[part, row],
+                    src_ref=source.at[source_rows, :],
+                    dst_ref=far_panel.at[part, row, held],
                     send_sem=panel_ssem.at[part, offset - 1],
                     recv_sem=panel_rsem.at[part, offset - 1],
                     device_id={"row": to},
@@ -235,14 +244,28 @@
             )
             panel_recvs.append(
                 pltpu.make_async_remote_copy(
-                    src_ref=source.at[here, :],
-                    dst_ref=far_panel.at[part, origin],
+                    src_ref=source.at[source_rows, :],
+                    dst_ref=far_panel.at[part, origin, held],
                     send_sem=panel_ssem.at[part, offset - 1],
                     recv_sem=panel_rsem.at[part, offset - 1],
                     device_id={"row": to},
                     device_id_type=MESH,
                 )
             )
+            for hop in range(1, shares):
+                giver = lax.rem(pole + shares - hop, shares)
+                theirs = pl.ds(pl.multiple_of(giver * height, height), height)
+                for rows_of, group in ((held, panel_passes), (theirs, passed_recvs)):
+                    group.append(
+                        pltpu.make_async_remote_copy(
+                            src_ref=far_panel.at[part, origin, held],
+                            dst_ref=far_panel.at[part, origin, rows_of],
+                            send_sem=pass_ssem.at[part, offset - 1, hop - 1],
+                            recv_sem=pass_rsem.at[part, offset - 1, hop - 1],
+                            device_id={"pole": lax.rem(pole + hop, shares)},
+                            device_id_type=MESH,
+                        )
+                    )
         theirs = pl.ds(pl.multiple_of(to * block, block), block)
         for part, source in enumerate((front_h, front_s)):
             front_sends.append(
@@ -274,6 +297,14 @@
     shift_imag = shift[0, 1]
     inverse = pivot_inverse(piv_v[0], piv_v[1], shift_real, shift_imag)
     inv_high, inv_low = split(inverse)
+    for copy in panel_recvs:
+        copy.wait_recv()
+    for copy in panel_passes:
+        copy.start()
+    for copy in panel_sends:
+        copy.wait_send()
+    for copy in front_sends:
+        copy.start()
     for copy in local[3:]:
         copy.wait()
     weight_real = weight[0, 0]
@@ -300,11 +331,7 @@
     anc_flipped = side((anc[0].T, anc[1].T))
     inv_below = jnp.concatenate([below(inv_high), below(inv_low)], axis=0)
 
-    for copy in panel_sends:
-        copy.wait_send()
-    for copy in front_sends:
-        copy.start()
-    for copy in panel_recvs:
+    for copy in passed_recvs:
         copy.wait_recv()
     far_coupling = side(
         couple(
@@ -372,19 +399,6 @@
     ]
     for copy in layer_copies:
         copy.start()
-
-    for copy in front_recvs:
-        copy.wait_recv()
-    for index in range(rows):
-        flag = pattern[index, row].astype(F32)
-        margin = far_front[1, index].astype(F32)
-        hamil = far_front[0, index].astype(F32)
-        at = slice(index * width, (index + 1) * width)
-        schur_v[0, index] = (flag * (hamil - shift_real * margin) - update[0][at]).astype(BF16)
-        schur_v[1, index] = (flag * (-shift_imag * margin) - update[1][at]).astype(BF16)
-
-    schur_copy = pltpu.make_async_copy(schur_v, schur_out, out_sem.at[0])
-    schur_copy.start()
 
     for copy in layer_copies:
         copy.wait_recv()
@@ -413,6 +427,19 @@
     for copy in last_copies:
         copy.start()
 
+    for copy in front_recvs:
+        copy.wait_recv()
+    for index in range(rows):
+        flag = pattern[index, row].astype(F32)
+        margin = far_front[1, index].astype(F32)
+        hamil = far_front[0, index].astype(F32)
+        at = slice(index * width, (index + 1) * width)
+        schur_v[0, index] = (flag * (hamil - shift_real * margin) - update[0][at]).astype(BF16)
+        schur_v[1, index] = (flag * (-shift_imag * margin) - update[1][at]).astype(BF16)
+
+    schur_copy = pltpu.make_async_copy(schur_v, schur_out, out_sem.at[0])
+    schur_copy.start()
+
     for copy in rows_copies:
         copy.wait_recv()
     rows_sum = part_rows[me]
@@ -424,25 +451,13 @@
 
     for copy in last_recvs:
         copy.wait_recv()
-    for copy in front_sends + piv_copies + rows_copies:
+    for copy in panel_passes + front_sends + piv_copies + rows_copies:
         copy.wait_send()
     for copy in layer_copies + last_copies:
         copy.wait_send()
     schur_copy.wait()
     rows_copy.wait()
     own_copy.wait()
-
-
-def hand_over(*refs):
-    sources, targets, sem = refs[:3], refs[3:6], refs[6]
-    copies = [
-        pltpu.make_async_copy(source, target, sem.at[index])
-        for index, (source, target) in enumerate(zip(sources, targets))
-    ]
-    for copy in copies:
-        copy.start()
-    for copy in copies:
-        copy.wait()
 
 
 def shards(
@@ -499,6 +514,8 @@
             pltpu.VMEM((layer - 1, strip, piece), BF16),
             pltpu.VMEM((strip, piece), BF16),
             pltpu.VMEM((rows - 1, strip, piece), BF16),
+            dma((2, rows - 1, poles - 1)),
+            dma((2, rows - 1, poles - 1)),
             dma((12,)),
             dma((2, rows - 1)),
             dma((2, rows - 1)),
@@ -530,15 +547,7 @@
         pivot_s,
         ancestor,
     )
-    schur, rows_out, pivot_out = pl.pallas_call(
-        hand_over,
-        out_shape=out_shape,
-        in_specs=[hbm] * 3,
-        out_specs=(hbm,) * 3,
-        scratch_shapes=[dma((3,))],
-        compiler_params=pltpu.CompilerParams(vmem_limit_bytes=60 * 1024 * 1024),
-        name="hand_over",
-    )(*found)
+    schur, rows_out, pivot_out = found
     return (
         schur.reshape(ancestor_inverse.shape),
         rows_out,

time: 43.1 us -> 29.3 us (0.68)
  Pallas kernels: 42.3 us -> 25.6 us
  local copies, waits for them, and re-layouts: 0 us -> 2.98 us
    pallas_call x1 -> x0, Pallas kernels: 14 us -> none  [shards(): pl.pallas_call(hand_over, out_shape=out_shape, in_specs=[hbm] * 3, out_sp...]
    unnamed x0 -> x7, local copies, waits for them, and re-layouts: none -> 2.98 us
    pallas_call x1, Pallas kernels: 28.3 us -> 25.6 us  [shards(): pl.pallas_call(functools.partial(step, rows, cols, poles), out_shape=out_...]
where the time goes in v3:
time: 29.3 us; the launch traced here: 29.2 us
  Pallas kernels  25.6 us (87%)
  local copies, waits for them, and re-layouts  2.98 us (10%)
  between operations  0.66 us (2%)
    pallas_call x1, Pallas kernels, shards(): pl.pallas_call(functools.partial(step, rows, cols, poles), out_shape=out_...  25.6 us
    unnamed x7, local copies, waits for them, and re-layouts  2.98 us

profile of v3, /device:TPU:0, one launch (start us, length us, event | category | flops | bytes accessed | tf_op | source)
XLA Modules:
  0.0 29.2 jit_solution(16135291060121786443)
XLA Ops:
  0.6 25.6 %front_step.1 = (bf16[2,4,64,256]{3,2,1,0:T(8,128)(2,1)}, f32[64,128]{1,0:T(8,128)}, f32[4,64,128]{2,1,0:T(8,128)}) custom-call(f32[1,2]{1,0:T(1,128)} %shift_hbm.1, f32[1,2]{1,0:T(1,128)} %weight_hbm.1, s32[4,4]{1,0:T(4,128)} %pattern_hbm.1, bf16[64,1024]{1,0:T(8,128)(2,1)} %front_h.1, bf16[64,1024]{1,0:T(8,128)(2,1)} %front_s.1, bf16[256,256]{1,0:T(8,128)(2,1)} %panel_h.1, ...), custom_call_target="tpu_custom_call" | custom-call | tf_op jit(solution)/shard_map/front_step/pallas_call | solution.py:492
  26.2 0.0 copy-start.1
  26.2 0.0 copy-start
  26.2 1.7 %copy.17 = bf16[1,2,4,1,64,256]{5,4,3,2,1,0:T(8,128)(2,1)} copy(bf16[1,2,4,1,64,256]{5,4,3,2,1,0:T(8,128)(2,1)} %bitcast.6) | data formatting | bytes 524288
  27.9 0.0 copy-done.1
  27.9 0.6 %copy.18 = f32[64,128]{1,0:T(8,128)} copy(f32[64,128]{1,0:T(8,128)S(1)} %copy-done.1) | data formatting | bytes 65536
  28.5 0.0 copy-done
  28.5 0.7 %copy.19 = f32[256,128]{1,0:T(8,128)} copy(f32[256,128]{1,0:T(8,128)S(1)} %bitcast.7) | data formatting | bytes 262144
Async XLA Ops:
  26.2 1.7 %copy-start.1 = (f32[64,128]{1,0:T(8,128)S(1)}, f32[64,128]{1,0:T(8,128)}, u32[]{:S(2)}) copy-start(f32[64,128]{1,0:T(8,128)} %get-tuple-element.16) | copy-start | bytes 98308
  26.2 2.3 %copy-start = (f32[4,64,128]{2,1,0:T(8,128)S(1)}, f32[4,64,128]{2,1,0:T(8,128)}, u32[]{:S(2)}) copy-start(f32[4,64,128]{2,1,0:T(8,128)} %get-tuple-element.8) | copy-start | bytes 393220

commit v4 on v3

--- a/solution.py
+++ b/solution.py
@@ -133,6 +133,7 @@
     pattern,
     piv_v,
     own_panel,
+    own_front,
     far_panel,
     far_front,
     anc_v,
@@ -198,24 +199,24 @@
         pltpu.make_async_copy(source, target, local_sem.at[index])
         for index, (source, target) in enumerate(
             [
+                (panel_h, own_panel.at[0]),
+                (panel_s, own_panel.at[1]),
                 (shift_hbm, shift),
                 (pivot_h, piv_v.at[0]),
                 (pivot_s, piv_v.at[1]),
+                (front_h, own_front.at[0]),
+                (front_s, own_front.at[1]),
                 (weight_hbm, weight),
                 (pattern_hbm, pattern),
-                (panel_h, own_panel.at[0]),
-                (panel_s, own_panel.at[1]),
                 (ancestor, anc_v),
-                (panel_h.at[here, :], far_panel.at[0, row]),
-                (panel_s.at[here, :], far_panel.at[1, row]),
-                (front_h.at[:, mine], far_front.at[0, row]),
-                (front_s.at[:, mine], far_front.at[1, row]),
             ]
         )
     ]
     for copy in local:
         copy.start()
     pl.semaphore_wait(barrier, rows - 1 + layer - 1)
+    for copy in local[:2]:
+        copy.wait()
 
     shares = poles if width % (16 * poles) == 0 else 1
     height = width // shares
@@ -231,59 +232,39 @@
     for offset in range(1, rows):
         to = row_peer(offset)
         origin = lax.rem(row + rows - offset, rows)
-        for part, source in enumerate((panel_h, panel_s)):
-            panel_sends.append(
+        for slot, group in ((row, panel_sends), (origin, panel_recvs)):
+            group.append(
                 pltpu.make_async_remote_copy(
-                    src_ref=source.at[source_rows, :],
-                    dst_ref=far_panel.at[part, row, held],
-                    send_sem=panel_ssem.at[part, offset - 1],
-                    recv_sem=panel_rsem.at[part, offset - 1],
+                    src_ref=own_panel.at[:, source_rows],
+                    dst_ref=far_panel.at[:, slot, held],
+                    send_sem=panel_ssem.at[offset - 1],
+                    recv_sem=panel_rsem.at[offset - 1],
                     device_id={"row": to},
                     device_id_type=MESH,
                 )
             )
-            panel_recvs.append(
+        for hop in range(1, shares):
+            giver = lax.rem(pole + shares - hop, shares)
+            theirs = pl.ds(pl.multiple_of(giver * height, height), height)
+            for rows_of, group in ((held, panel_passes), (theirs, passed_recvs)):
+                group.append(
+                    pltpu.make_async_remote_copy(
+                        src_ref=far_panel.at[:, origin, held],
+                        dst_ref=far_panel.at[:, origin, rows_of],
+                        send_sem=pass_ssem.at[offset - 1, hop - 1],
+                        recv_sem=pass_rsem.at[offset - 1, hop - 1],
+                        device_id={"pole": lax.rem(pole + hop, shares)},
+                        device_id_type=MESH,
+                    )
+                )
+        theirs = pl.ds(pl.multiple_of(to * block, block), block)
+        for slot, group in ((row, front_sends), (origin, front_recvs)):
+            group.append(
                 pltpu.make_async_remote_copy(
-                    src_ref=source.at[source_rows, :],
-                    dst_ref=far_panel.at[part, origin, held],
-                    send_sem=panel_ssem.at[part, offset - 1],
-                    recv_sem=panel_rsem.at[part, offset - 1],
-                    device_id={"row": to},
-                    device_id_type=MESH,
-                )
-            )
-            for hop in range(1, shares):
-                giver = lax.rem(pole + shares - hop, shares)
-                theirs = pl.ds(pl.multiple_of(giver * height, height), height)
-                for rows_of, group in ((held, panel_passes), (theirs, passed_recvs)):
-                    group.append(
-                        pltpu.make_async_remote_copy(
-                            src_ref=far_panel.at[part, origin, held],
-                            dst_ref=far_panel.at[part, origin, rows_of],
-                            send_sem=pass_ssem.at[part, offset - 1, hop - 1],
-                            recv_sem=pass_rsem.at[part, offset - 1, hop - 1],
-                            device_id={"pole": lax.rem(pole + hop, shares)},
-                            device_id_type=MESH,
-                        )
-                    )
-        theirs = pl.ds(pl.multiple_of(to * block, block), block)
-        for part, source in enumerate((front_h, front_s)):
-            front_sends.append(
-                pltpu.make_async_remote_copy(
-                    src_ref=source.at[:, theirs],
-                    dst_ref=far_front.at[part, row],
-                    send_sem=front_ssem.at[part, offset - 1],
-                    recv_sem=front_rsem.at[part, offset - 1],
-                    device_id={"row": to},
-                    device_id_type=MESH,
-                )
-            )
-            front_recvs.append(
-                pltpu.make_async_remote_copy(
-                    src_ref=source.at[:, theirs],
-                    dst_ref=far_front.at[part, origin],
-                    send_sem=front_ssem.at[part, offset - 1],
-                    recv_sem=front_rsem.at[part, offset - 1],
+                    src_ref=own_front.at[:, :, theirs],
+                    dst_ref=far_front.at[:, slot],
+                    send_sem=front_ssem.at[offset - 1],
+                    recv_sem=front_rsem.at[offset - 1],
                     device_id={"row": to},
                     device_id_type=MESH,
                 )
@@ -291,7 +272,7 @@
     for copy in panel_sends:
         copy.start()
 
-    for copy in local[:3]:
+    for copy in local[2:5]:
         copy.wait()
     shift_real = shift[0, 0]
     shift_imag = shift[0, 1]
@@ -303,10 +284,12 @@
         copy.start()
     for copy in panel_sends:
         copy.wait_send()
+    for copy in local[5:]:
+        copy.wait()
     for copy in front_sends:
         copy.start()
-    for copy in local[3:]:
-        copy.wait()
+    far_panel[:, row] = own_panel[:, here]
+    far_front[:, row] = own_front[:, :, mine]
     weight_real = weight[0, 0]
     weight_imag = weight[0, 1]
     coupling = couple(own_panel[0], own_panel[1], shift_real, shift_imag)
@@ -376,7 +359,6 @@
     part = halves(nn(anc_flipped, below(solved)))
     weighted_imag = -(weight_real * part[1] + weight_imag * part[0])
     scatter(weighted_imag, part_rows, send_rows, width)
-    rows_copies = exchange(send_rows, recv_rows, rows_ssem, rows_rsem)
 
     update = halves(nt(side(solved), coupling_across))
 
@@ -399,6 +381,7 @@
     ]
     for copy in layer_copies:
         copy.start()
+    rows_copies = exchange(send_rows, recv_rows, rows_ssem, rows_rsem)
 
     for copy in layer_copies:
         copy.wait_recv()
@@ -449,15 +432,34 @@
     rows_copy = pltpu.make_async_copy(final_rows, rows_out, out_sem.at[1])
     rows_copy.start()
 
-    for copy in last_recvs:
-        copy.wait_recv()
-    for copy in panel_passes + front_sends + piv_copies + rows_copies:
-        copy.wait_send()
-    for copy in layer_copies + last_copies:
+    for copy in panel_passes + front_sends + piv_copies + layer_copies + rows_copies:
         copy.wait_send()
     schur_copy.wait()
     rows_copy.wait()
     own_copy.wait()
+    for copy in last_copies:
+        copy.wait_send()
+    for copy in last_recvs:
+        copy.wait_recv()
+
+
+def hand_over(*refs):
+    sources, targets, staged, sems = refs[:3], refs[3:6], refs[6:9], refs[9]
+    inward = []
+    outward = []
+    for index in range(3):
+        inward.append(
+            pltpu.make_async_copy(sources[index], staged[index], sems.at[0, index])
+        )
+        outward.append(
+            pltpu.make_async_copy(staged[index], targets[index], sems.at[1, index])
+        )
+        inward[index].start()
+    for index in range(3):
+        inward[index].wait()
+        outward[index].start()
+    for copy in outward:
+        copy.wait()
 
 
 def shards(
@@ -500,6 +502,7 @@
             pltpu.SMEM(pattern.shape, jnp.int32),
             pltpu.VMEM((2, size, size), BF16),
             pltpu.VMEM((2, block, size), BF16),
+            pltpu.VMEM((2,) + front_h.shape, BF16),
             pltpu.VMEM((2, rows, width, size), BF16),
             pltpu.VMEM((2, rows, width, block), BF16),
             pltpu.VMEM((2, rows, width, block), BF16),
@@ -514,13 +517,13 @@
             pltpu.VMEM((layer - 1, strip, piece), BF16),
             pltpu.VMEM((strip, piece), BF16),
             pltpu.VMEM((rows - 1, strip, piece), BF16),
-            dma((2, rows - 1, poles - 1)),
-            dma((2, rows - 1, poles - 1)),
-            dma((12,)),
-            dma((2, rows - 1)),
-            dma((2, rows - 1)),
-            dma((2, rows - 1)),
-            dma((2, rows - 1)),
+            dma((rows - 1, poles - 1)),
+            dma((rows - 1, poles - 1)),
+            dma((10,)),
+            dma((rows - 1,)),
+            dma((rows - 1,)),
+            dma((rows - 1,)),
+            dma((rows - 1,)),
             dma((layer - 1,)),
             dma((layer - 1,)),
             dma((layer - 1,)),
@@ -547,7 +550,16 @@
         pivot_s,
         ancestor,
     )
-    schur, rows_out, pivot_out = found
+    schur, rows_out, pivot_out = pl.pallas_call(
+        hand_over,
+        out_shape=out_shape,
+        in_specs=[hbm] * 3,
+        out_specs=(hbm,) * 3,
+        scratch_shapes=[pltpu.VMEM(part.shape, part.dtype) for part in out_shape]
+        + [dma((2, 3))],
+        compiler_params=pltpu.CompilerParams(vmem_limit_bytes=60 * 1024 * 1024),
+        name="hand_over",
+    )(*found)
     return (
         schur.reshape(ancestor_inverse.shape),
         rows_out,

time: 29.3 us -> 27.7 us (0.945)
  local copies, waits for them, and re-layouts: 2.98 us -> 0 us
  Pallas kernels: 25.6 us -> 26.9 us
    unnamed x7 -> x0, local copies, waits for them, and re-layouts: 2.98 us -> none
    pallas_call x0 -> x1, Pallas kernels: none -> 1.75 us  [shards(): pl.pallas_call(hand_over, out_shape=out_shape, in_specs=[hbm] * 3, out_sp...]
    pallas_call x1, Pallas kernels: 25.6 us -> 25.1 us  [shards(): pl.pallas_call(functools.partial(step, rows, cols, poles), out_shape=out_...]
where the time goes in v4:
time: 27.7 us; the launch traced here: 27.5 us
  Pallas kernels  26.9 us (97%)
  between operations  0.64 us (2%)
    pallas_call x1, Pallas kernels, shards(): pl.pallas_call(functools.partial(step, rows, cols, poles), out_shape=out_...  25.1 us
    pallas_call x1, Pallas kernels, shards(): pl.pallas_call(hand_over, out_shape=out_shape, in_specs=[hbm] * 3, out_sp...  1.75 us

profile of v4, /device:TPU:0, one launch (start us, length us, event | category | flops | bytes accessed | tf_op | source)
XLA Modules:
  0.0 27.5 jit_solution(16117765331552065020)
XLA Ops:
  0.6 25.1 %front_step.1 = (bf16[2,4,64,256]{3,2,1,0:T(8,128)(2,1)}, f32[64,128]{1,0:T(8,128)}, f32[4,64,128]{2,1,0:T(8,128)}) custom-call(f32[1,2]{1,0:T(1,128)} %shift_hbm.1, f32[1,2]{1,0:T(1,128)} %weight_hbm.1, s32[4,4]{1,0:T(4,128)} %pattern_hbm.1, bf16[64,1024]{1,0:T(8,128)(2,1)} %front_h.1, bf16[64,1024]{1,0:T(8,128)(2,1)} %front_s.1, bf16[256,256]{1,0:T(8,128)(2,1)} %panel_h.1, ...), custom_call_target="tpu_custom_call" | custom-call | tf_op jit(solution)/shard_map/front_step/pallas_call | solution.py:494
  25.8 1.8 %hand_over.1 = (bf16[2,4,64,256]{3,2,1,0:T(8,128)(2,1)}, f32[64,128]{1,0:T(8,128)}, f32[4,64,128]{2,1,0:T(8,128)}) custom-call(bf16[2,4,64,256]{3,2,1,0:T(8,128)(2,1)} %get-tuple-element.9.refs_0_, f32[64,128]{1,0:T(8,128)} %get-tuple-element.10.refs_1_, f32[4,64,128]{2,1,0:T(8,128)} %get-tuple-element.11.refs_2_), custom_call_target="tpu_custom_call" | custom-call | tf_op jit(solution)/shard_map/hand_over/pallas_call | solution.py:553

commit v5 on v4

--- a/solution.py
+++ b/solution.py
@@ -43,10 +43,6 @@
     return halves(nn(side(left), below(right)))
 
 
-def product_nt(left, right):
-    return halves(nt(side(left), across(right)))
-
-
 def rounded(pair):
     return pair[0].astype(BF16), pair[1].astype(BF16)
 
@@ -67,7 +63,7 @@
     return real.astype(BF16), (-shift_imag * margin).astype(BF16)
 
 
-def pivot_inverse(pivot_h, pivot_s, shift_real, shift_imag):
+def pivot_inverse(pivot_h, pivot_s, shift_real, shift_imag, meanwhile):
     size = pivot_h.shape[0]
     margin = pivot_s.astype(F32)
     real = pivot_h.astype(F32) - shift_real * margin
@@ -104,6 +100,7 @@
     )
     eighth_b = rounded(halves(tall[:size]))
     total = plus(total, halves(tall[size:]))
+    meanwhile()
     total = plus(total, product(rounded(total), eighth_b))
     return (
         total[0] * right_real - total[1] * right_imag,
@@ -276,43 +273,39 @@
         copy.wait()
     shift_real = shift[0, 0]
     shift_imag = shift[0, 1]
-    inverse = pivot_inverse(piv_v[0], piv_v[1], shift_real, shift_imag)
+
+    def pass_on():
+        for copy in panel_recvs:
+            copy.wait_recv()
+        for copy in panel_passes:
+            copy.start()
+        for copy in panel_sends:
+            copy.wait_send()
+        for copy in local[5:7]:
+            copy.wait()
+        for copy in front_sends:
+            copy.start()
+
+    inverse = pivot_inverse(piv_v[0], piv_v[1], shift_real, shift_imag, pass_on)
     inv_high, inv_low = split(inverse)
-    for copy in panel_recvs:
-        copy.wait_recv()
-    for copy in panel_passes:
-        copy.start()
-    for copy in panel_sends:
-        copy.wait_send()
-    for copy in local[5:]:
+    inv_below = jnp.concatenate([below(inv_high), below(inv_low)], axis=0)
+    for copy in local[7:]:
         copy.wait()
-    for copy in front_sends:
-        copy.start()
-    far_panel[:, row] = own_panel[:, here]
-    far_front[:, row] = own_front[:, :, mine]
     weight_real = weight[0, 0]
     weight_imag = weight[0, 1]
     coupling = couple(own_panel[0], own_panel[1], shift_real, shift_imag)
-    coupling_across = across(coupling)
-    flipped = rounded(
-        halves(nt(side(inv_high), coupling_across) + nt(side(inv_low), coupling_across))
-    )
+    coupled = side(coupling)
+    own_solved = rounded(halves(nn(side((coupled, coupled)), inv_below)))
     anc = (
         anc_v[0].reshape(rows * width, block),
         anc_v[1].reshape(rows * width, block),
     )
-    swept = product_nt(flipped, anc)
-    swept_both = side(
-        rounded(
-            (
-                weight_real * swept[1] + weight_imag * swept[0],
-                weight_real * swept[0] - weight_imag * swept[1],
-            )
-        )
-    )
+    swept = product(anc, own_solved)
+    swept_imag = (weight_real * swept[1] + weight_imag * swept[0]).astype(BF16)
+    swept_real = (weight_real * swept[0] - weight_imag * swept[1]).astype(BF16)
+    swept_both = side((swept_imag.T, swept_real.T))
     own_share = (weight_real * inverse[1] + weight_imag * inverse[0]) * (1.0 / (rows * cols))
-    anc_flipped = side((anc[0].T, anc[1].T))
-    inv_below = jnp.concatenate([below(inv_high), below(inv_low)], axis=0)
+    far_panel[:, row] = own_panel[:, here]
 
     for copy in passed_recvs:
         copy.wait_recv()
@@ -356,11 +349,12 @@
     share = own_share + nn(swept_both, jnp.concatenate(solved, axis=0))
     scatter(share, part_piv, send_piv, strip)
     piv_copies = exchange(send_piv, recv_piv, piv_ssem, piv_rsem)
-    part = halves(nn(anc_flipped, below(solved)))
+    part = halves(nn(side((anc[0].T, anc[1].T)), below(solved)))
     weighted_imag = -(weight_real * part[1] + weight_imag * part[0])
     scatter(weighted_imag, part_rows, send_rows, width)
 
-    update = halves(nt(side(solved), coupling_across))
+    update = halves(nt(side(solved), across(coupling)))
+    far_front[:, row] = own_front[:, :, mine]
 
     for copy in piv_copies:
         copy.wait_recv()

time: 27.7 us -> 27.6 us (level)
  no operation moved by 1% of the time
where the time goes in v5:
time: 27.6 us; the launch traced here: 27.5 us
  Pallas kernels  26.9 us (97%)
  between operations  0.64 us (2%)
    pallas_call x1, Pallas kernels, shards(): pl.pallas_call(functools.partial(step, rows, cols, poles), out_shape=out_...  25.1 us
    pallas_call x1, Pallas kernels, shards(): pl.pallas_call(hand_over, out_shape=out_shape, in_specs=[hbm] * 3, out_sp...  1.75 us

profile of v5, /device:TPU:0, one launch (start us, length us, event | category | flops | bytes accessed | tf_op | source)
XLA Modules:
  0.0 27.5 jit_solution(4156202722500331948)
XLA Ops:
  0.6 25.1 %front_step.1 = (bf16[2,4,64,256]{3,2,1,0:T(8,128)(2,1)}, f32[64,128]{1,0:T(8,128)}, f32[4,64,128]{2,1,0:T(8,128)}) custom-call(f32[1,2]{1,0:T(1,128)} %shift_hbm.1, f32[1,2]{1,0:T(1,128)} %weight_hbm.1, s32[4,4]{1,0:T(4,128)} %pattern_hbm.1, bf16[64,1024]{1,0:T(8,128)(2,1)} %front_h.1, bf16[64,1024]{1,0:T(8,128)(2,1)} %front_s.1, bf16[256,256]{1,0:T(8,128)(2,1)} %panel_h.1, ...), custom_call_target="tpu_custom_call" | custom-call | tf_op jit(solution)/shard_map/front_step/pallas_call | solution.py:488
  25.7 1.8 %hand_over.1 = (bf16[2,4,64,256]{3,2,1,0:T(8,128)(2,1)}, f32[64,128]{1,0:T(8,128)}, f32[4,64,128]{2,1,0:T(8,128)}) custom-call(bf16[2,4,64,256]{3,2,1,0:T(8,128)(2,1)} %get-tuple-element.9.refs_0_, f32[64,128]{1,0:T(8,128)} %get-tuple-element.10.refs_1_, f32[4,64,128]{2,1,0:T(8,128)} %get-tuple-element.11.refs_2_), custom_call_target="tpu_custom_call" | custom-call | tf_op jit(solution)/shard_map/hand_over/pallas_call | solution.py:547

commit v6 on v5

--- a/solution.py
+++ b/solution.py
@@ -147,6 +147,8 @@
     layer_recv,
     pass_ssem,
     pass_rsem,
+    move_ssem,
+    move_rsem,
     local_sem,
     panel_ssem,
     panel_rsem,
@@ -224,6 +226,8 @@
     panel_recvs = []
     panel_passes = []
     passed_recvs = []
+    front_passes = []
+    moved_recvs = []
     front_sends = []
     front_recvs = []
     for offset in range(1, rows):
@@ -243,23 +247,27 @@
         for hop in range(1, shares):
             giver = lax.rem(pole + shares - hop, shares)
             theirs = pl.ds(pl.multiple_of(giver * height, height), height)
-            for rows_of, group in ((held, panel_passes), (theirs, passed_recvs)):
-                group.append(
-                    pltpu.make_async_remote_copy(
-                        src_ref=far_panel.at[:, origin, held],
-                        dst_ref=far_panel.at[:, origin, rows_of],
-                        send_sem=pass_ssem.at[offset - 1, hop - 1],
-                        recv_sem=pass_rsem.at[offset - 1, hop - 1],
-                        device_id={"pole": lax.rem(pole + hop, shares)},
-                        device_id_type=MESH,
+            for array, ssem, rsem, sends, recvs in (
+                (far_panel, pass_ssem, pass_rsem, panel_passes, passed_recvs),
+                (far_front, move_ssem, move_rsem, front_passes, moved_recvs),
+            ):
+                for rows_of, group in ((held, sends), (theirs, recvs)):
+                    group.append(
+                        pltpu.make_async_remote_copy(
+                            src_ref=array.at[:, origin, held],
+                            dst_ref=array.at[:, origin, rows_of],
+                            send_sem=ssem.at[offset - 1, hop - 1],
+                            recv_sem=rsem.at[offset - 1, hop - 1],
+                            device_id={"pole": lax.rem(pole + hop, shares)},
+                            device_id_type=MESH,
+                        )
                     )
-                )
         theirs = pl.ds(pl.multiple_of(to * block, block), block)
         for slot, group in ((row, front_sends), (origin, front_recvs)):
             group.append(
                 pltpu.make_async_remote_copy(
-                    src_ref=own_front.at[:, :, theirs],
-                    dst_ref=far_front.at[:, slot],
+                    src_ref=own_front.at[:, held, theirs],
+                    dst_ref=far_front.at[:, slot, held],
                     send_sem=front_ssem.at[offset - 1],
                     recv_sem=front_rsem.at[offset - 1],
                     device_id={"row": to},
@@ -374,6 +382,10 @@
         for offset in range(1, rows)
     ]
     for copy in layer_copies:
+        copy.start()
+    for copy in front_recvs:
+        copy.wait_recv()
+    for copy in front_passes:
         copy.start()
     rows_copies = exchange(send_rows, recv_rows, rows_ssem, rows_rsem)
 
@@ -404,7 +416,7 @@
     for copy in last_copies:
         copy.start()
 
-    for copy in front_recvs:
+    for copy in moved_recvs:
         copy.wait_recv()
     for index in range(rows):
         flag = pattern[index, row].astype(F32)
@@ -426,7 +438,7 @@
     rows_copy = pltpu.make_async_copy(final_rows, rows_out, out_sem.at[1])
     rows_copy.start()
 
-    for copy in panel_passes + front_sends + piv_copies + layer_copies + rows_copies:
+    for copy in panel_passes + front_sends + front_passes + piv_copies + layer_copies + rows_copies:
         copy.wait_send()
     schur_copy.wait()
     rows_copy.wait()
@@ -511,6 +523,8 @@
             pltpu.VMEM((layer - 1, strip, piece), BF16),
             pltpu.VMEM((strip, piece), BF16),
             pltpu.VMEM((rows - 1, strip, piece), BF16),
+            dma((rows - 1, poles - 1)),
+            dma((rows - 1, poles - 1)),
             dma((rows - 1, poles - 1)),
             dma((rows - 1, poles - 1)),
             dma((10,)),

time: 27.6 us -> 27.7 us (level)
  no operation moved by 1% of the time
where the time goes in v6:
time: 27.7 us; the launch traced here: 27.5 us
  Pallas kernels  26.9 us (97%)
  between operations  0.64 us (2%)
    pallas_call x1, Pallas kernels, shards(): pl.pallas_call(functools.partial(step, rows, cols, poles), out_shape=out_...  25.1 us
    pallas_call x1, Pallas kernels, shards(): pl.pallas_call(hand_over, out_shape=out_shape, in_specs=[hbm] * 3, out_sp...  1.75 us

profile of v6, /device:TPU:0, one launch (start us, length us, event | category | flops | bytes accessed | tf_op | source)
XLA Modules:
  0.0 27.5 jit_solution(15760573953983390079)
XLA Ops:
  0.6 25.1 %front_step.1 = (bf16[2,4,64,256]{3,2,1,0:T(8,128)(2,1)}, f32[64,128]{1,0:T(8,128)}, f32[4,64,128]{2,1,0:T(8,128)}) custom-call(f32[1,2]{1,0:T(1,128)} %shift_hbm.1, f32[1,2]{1,0:T(1,128)} %weight_hbm.1, s32[4,4]{1,0:T(4,128)} %pattern_hbm.1, bf16[64,1024]{1,0:T(8,128)(2,1)} %front_h.1, bf16[64,1024]{1,0:T(8,128)(2,1)} %front_s.1, bf16[256,256]{1,0:T(8,128)(2,1)} %panel_h.1, ...), custom_call_target="tpu_custom_call" | custom-call | tf_op jit(solution)/shard_map/front_step/pallas_call | solution.py:500
  25.8 1.8 %hand_over.1 = (bf16[2,4,64,256]{3,2,1,0:T(8,128)(2,1)}, f32[64,128]{1,0:T(8,128)}, f32[4,64,128]{2,1,0:T(8,128)}) custom-call(bf16[2,4,64,256]{3,2,1,0:T(8,128)(2,1)} %get-tuple-element.9.refs_0_, f32[64,128]{1,0:T(8,128)} %get-tuple-element.10.refs_1_, f32[4,64,128]{2,1,0:T(8,128)} %get-tuple-element.11.refs_2_), custom_call_target="tpu_custom_call" | custom-call | tf_op jit(solution)/shard_map/hand_over/pallas_call | solution.py:561

commit v7 on v5

--- a/solution.py
+++ b/solution.py
@@ -351,10 +351,7 @@
     piv_copies = exchange(send_piv, recv_piv, piv_ssem, piv_rsem)
     part = halves(nn(side((anc[0].T, anc[1].T)), below(solved)))
     weighted_imag = -(weight_real * part[1] + weight_imag * part[0])
-    scatter(weighted_imag, part_rows, send_rows, width)
-
-    update = halves(nt(side(solved), across(coupling)))
-    far_front[:, row] = own_front[:, :, mine]
+
 
     for copy in piv_copies:
         copy.wait_recv()
@@ -375,7 +372,10 @@
     ]
     for copy in layer_copies:
         copy.start()
+    scatter(weighted_imag, part_rows, send_rows, width)
     rows_copies = exchange(send_rows, recv_rows, rows_ssem, rows_rsem)
+    update = halves(nt(side(solved), across(coupling)))
+    far_front[:, row] = own_front[:, :, mine]
 
     for copy in layer_copies:
         copy.wait_recv()
@@ -439,17 +439,20 @@
 
 def hand_over(*refs):
     sources, targets, staged, sems = refs[:3], refs[3:6], refs[6:9], refs[9]
+    half = sources[0].shape[1] // 2
+    pieces = [
+        (0, (part, pl.ds(start * half, half))) for part in range(2) for start in range(2)
+    ] + [(2, ()), (1, ())]
     inward = []
     outward = []
-    for index in range(3):
-        inward.append(
-            pltpu.make_async_copy(sources[index], staged[index], sems.at[0, index])
-        )
-        outward.append(
-            pltpu.make_async_copy(staged[index], targets[index], sems.at[1, index])
-        )
+    for index, (which, at) in enumerate(pieces):
+        source, stage, target = sources[which], staged[which], targets[which]
+        if at:
+            source, stage, target = source.at[at], stage.at[at], target.at[at]
+        inward.append(pltpu.make_async_copy(source, stage, sems.at[0, index]))
+        outward.append(pltpu.make_async_copy(stage, target, sems.at[1, index]))
         inward[index].start()
-    for index in range(3):
+    for index in range(len(pieces)):
         inward[index].wait()
         outward[index].start()
     for copy in outward:
@@ -550,7 +553,7 @@
         in_specs=[hbm] * 3,
         out_specs=(hbm,) * 3,
         scratch_shapes=[pltpu.VMEM(part.shape, part.dtype) for part in out_shape]
-        + [dma((2, 3))],
+        + [dma((2, 6))],
         compiler_params=pltpu.CompilerParams(vmem_limit_bytes=60 * 1024 * 1024),
         name="hand_over",
     )(*found)

time: 27.6 us -> 27.8 us (level)
  no operation moved by 1% of the time
where the time goes in v7:
time: 27.8 us; the launch traced here: 27.7 us
  Pallas kernels  27 us (97%)
  between operations  0.64 us (2%)
    pallas_call x1, Pallas kernels, shards(): pl.pallas_call(functools.partial(step, rows, cols, poles), out_shape=out_...  25.2 us
    pallas_call x1, Pallas kernels, shards(): pl.pallas_call(hand_over, out_shape=out_shape, in_specs=[hbm] * 3, out_sp...  1.8 us

profile of v7, /device:TPU:0, one launch (start us, length us, event | category | flops | bytes accessed | tf_op | source)
XLA Modules:
  0.0 27.7 jit_solution(16827497936638250183)
XLA Ops:
  0.6 25.2 %front_step.1 = (bf16[2,4,64,256]{3,2,1,0:T(8,128)(2,1)}, f32[64,128]{1,0:T(8,128)}, f32[4,64,128]{2,1,0:T(8,128)}) custom-call(f32[1,2]{1,0:T(1,128)} %shift_hbm.1, f32[1,2]{1,0:T(1,128)} %weight_hbm.1, s32[4,4]{1,0:T(4,128)} %pattern_hbm.1, bf16[64,1024]{1,0:T(8,128)(2,1)} %front_h.1, bf16[64,1024]{1,0:T(8,128)(2,1)} %front_s.1, bf16[256,256]{1,0:T(8,128)(2,1)} %panel_h.1, ...), custom_call_target="tpu_custom_call" | custom-call | tf_op jit(solution)/shard_map/front_step/pallas_call | solution.py:491
  25.9 1.8 %hand_over.1 = (bf16[2,4,64,256]{3,2,1,0:T(8,128)(2,1)}, f32[64,128]{1,0:T(8,128)}, f32[4,64,128]{2,1,0:T(8,128)}) custom-call(bf16[2,4,64,256]{3,2,1,0:T(8,128)(2,1)} %get-tuple-element.9.refs_0_, f32[64,128]{1,0:T(8,128)} %get-tuple-element.10.refs_1_, f32[4,64,128]{2,1,0:T(8,128)} %get-tuple-element.11.refs_2_), custom_call_target="tpu_custom_call" | custom-call | tf_op jit(solution)/shard_map/hand_over/pallas_call | solution.py:550

commit v8 on v5

--- a/solution.py
+++ b/solution.py
@@ -88,12 +88,11 @@
         -(left_real * imag + left_imag * real),
     )
     first_b = rounded(first)
-    first_below = below(first_b)
-    second = halves(nn(side(first_b), first_below))
+    second = product(first_b, first_b)
     second_b = rounded(second)
-    wide = nn(side(second_b), jnp.concatenate([first_below, below(second_b)], axis=1))
-    third = halves(wide[:, : 2 * size])
-    fourth_b = rounded(halves(wide[:, 2 * size :]))
+    tall = nn(jnp.concatenate([side(first_b), side(second_b)], axis=0), below(second_b))
+    third = halves(tall[:size])
+    fourth_b = rounded(halves(tall[size:]))
     total = plus(plus((identity + first[0], first[1]), second), third)
     tall = nn(
         jnp.concatenate([side(fourth_b), side(rounded(total))], axis=0), below(fourth_b)
@@ -215,7 +214,7 @@
     for copy in local[:2]:
         copy.wait()
 
-    shares = poles if width % (16 * poles) == 0 else 1
+    shares = 1
     height = width // shares
     first = pl.multiple_of(pole * height if shares > 1 else 0, height)
     held = pl.ds(first, height)
@@ -275,10 +274,6 @@
     shift_imag = shift[0, 1]
 
     def pass_on():
-        for copy in panel_recvs:
-            copy.wait_recv()
-        for copy in panel_passes:
-            copy.start()
         for copy in panel_sends:
             copy.wait_send()
         for copy in local[5:7]:
@@ -295,7 +290,7 @@
     weight_imag = weight[0, 1]
     coupling = couple(own_panel[0], own_panel[1], shift_real, shift_imag)
     coupled = side(coupling)
-    own_solved = rounded(halves(nn(side((coupled, coupled)), inv_below)))
+    own_solved = rounded(halves(nn(coupled, inv_below[: 2 * size])))
     anc = (
         anc_v[0].reshape(rows * width, block),
         anc_v[1].reshape(rows * width, block),
@@ -307,7 +302,7 @@
     own_share = (weight_real * inverse[1] + weight_imag * inverse[0]) * (1.0 / (rows * cols))
     far_panel[:, row] = own_panel[:, here]
 
-    for copy in passed_recvs:
+    for copy in panel_recvs:
         copy.wait_recv()
     far_coupling = side(
         couple(

time: 27.6 us -> 30.5 us (1.11)
  Pallas kernels: 26.9 us -> 29.7 us
    pallas_call x1, Pallas kernels: 25.1 us -> 28 us  [shards(): pl.pallas_call(functools.partial(step, rows, cols, poles), out_shape=out_...]
where the time goes in v8:
time: 30.5 us; the launch traced here: 30.4 us
  Pallas kernels  29.7 us (97%)
  between operations  0.64 us (2%)
    pallas_call x1, Pallas kernels, shards(): pl.pallas_call(functools.partial(step, rows, cols, poles), out_shape=out_...  28 us
    pallas_call x1, Pallas kernels, shards(): pl.pallas_call(hand_over, out_shape=out_shape, in_specs=[hbm] * 3, out_sp...  1.75 us

profile of v8, /device:TPU:0, one launch (start us, length us, event | category | flops | bytes accessed | tf_op | source)
XLA Modules:
  0.0 30.4 jit_solution(4760274406384387812)
XLA Ops:
  0.6 28.0 %front_step.1 = (bf16[2,4,64,256]{3,2,1,0:T(8,128)(2,1)}, f32[64,128]{1,0:T(8,128)}, f32[4,64,128]{2,1,0:T(8,128)}) custom-call(f32[1,2]{1,0:T(1,128)} %shift_hbm.1, f32[1,2]{1,0:T(1,128)} %weight_hbm.1, s32[4,4]{1,0:T(4,128)} %pattern_hbm.1, bf16[64,1024]{1,0:T(8,128)(2,1)} %front_h.1, bf16[64,1024]{1,0:T(8,128)(2,1)} %front_s.1, bf16[256,256]{1,0:T(8,128)(2,1)} %panel_h.1, ...), custom_call_target="tpu_custom_call" | custom-call | tf_op jit(solution)/shard_map/front_step/pallas_call | solution.py:483
  28.6 1.8 %hand_over.1 = (bf16[2,4,64,256]{3,2,1,0:T(8,128)(2,1)}, f32[64,128]{1,0:T(8,128)}, f32[4,64,128]{2,1,0:T(8,128)}) custom-call(bf16[2,4,64,256]{3,2,1,0:T(8,128)(2,1)} %get-tuple-element.9.refs_0_, f32[64,128]{1,0:T(8,128)} %get-tuple-element.10.refs_1_, f32[4,64,128]{2,1,0:T(8,128)} %get-tuple-element.11.refs_2_), custom_call_target="tpu_custom_call" | custom-call | tf_op jit(solution)/shard_map/hand_over/pallas_call | solution.py:542

commit v9 on v8

--- a/solution.py
+++ b/solution.py
@@ -214,7 +214,7 @@
     for copy in local[:2]:
         copy.wait()
 
-    shares = 1
+    shares = poles if width % (16 * poles) == 0 else 1
     height = width // shares
     first = pl.multiple_of(pole * height if shares > 1 else 0, height)
     held = pl.ds(first, height)
@@ -274,6 +274,10 @@
     shift_imag = shift[0, 1]
 
     def pass_on():
+        for index, copy in enumerate(panel_recvs):
+            copy.wait_recv()
+            for passed in panel_passes[index * (shares - 1) : (index + 1) * (shares - 1)]:
+                passed.start()
         for copy in panel_sends:
             copy.wait_send()
         for copy in local[5:7]:
@@ -290,7 +294,7 @@
     weight_imag = weight[0, 1]
     coupling = couple(own_panel[0], own_panel[1], shift_real, shift_imag)
     coupled = side(coupling)
-    own_solved = rounded(halves(nn(coupled, inv_below[: 2 * size])))
+    own_solved = rounded(halves(nn(side((coupled, coupled)), inv_below)))
     anc = (
         anc_v[0].reshape(rows * width, block),
         anc_v[1].reshape(rows * width, block),
@@ -302,7 +306,7 @@
     own_share = (weight_real * inverse[1] + weight_imag * inverse[0]) * (1.0 / (rows * cols))
     far_panel[:, row] = own_panel[:, here]
 
-    for copy in panel_recvs:
+    for copy in passed_recvs:
         copy.wait_recv()
     far_coupling = side(
         couple(

time: 30.5 us -> 27.2 us (0.89)
  Pallas kernels: 29.7 us -> 26.4 us
    pallas_call x1, Pallas kernels: 28 us -> 24.6 us  [shards(): pl.pallas_call(functools.partial(step, rows, cols, poles), out_shape=out_...]
where the time goes in v9:
time: 27.2 us; the launch traced here: 27 us
  Pallas kernels  26.4 us (97%)
  between operations  0.64 us (2%)
    pallas_call x1, Pallas kernels, shards(): pl.pallas_call(functools.partial(step, rows, cols, poles), out_shape=out_...  24.6 us
    pallas_call x1, Pallas kernels, shards(): pl.pallas_call(hand_over, out_shape=out_shape, in_specs=[hbm] * 3, out_sp...  1.75 us

profile of v9, /device:TPU:0, one launch (start us, length us, event | category | flops | bytes accessed | tf_op | source)
XLA Modules:
  0.0 27.0 jit_solution(11149419262654235900)
XLA Ops:
  0.6 24.6 %front_step.1 = (bf16[2,4,64,256]{3,2,1,0:T(8,128)(2,1)}, f32[64,128]{1,0:T(8,128)}, f32[4,64,128]{2,1,0:T(8,128)}) custom-call(f32[1,2]{1,0:T(1,128)} %shift_hbm.1, f32[1,2]{1,0:T(1,128)} %weight_hbm.1, s32[4,4]{1,0:T(4,128)} %pattern_hbm.1, bf16[64,1024]{1,0:T(8,128)(2,1)} %front_h.1, bf16[64,1024]{1,0:T(8,128)(2,1)} %front_s.1, bf16[256,256]{1,0:T(8,128)(2,1)} %panel_h.1, ...), custom_call_target="tpu_custom_call" | custom-call | tf_op jit(solution)/shard_map/front_step/pallas_call | solution.py:487
  25.3 1.8 %hand_over.1 = (bf16[2,4,64,256]{3,2,1,0:T(8,128)(2,1)}, f32[64,128]{1,0:T(8,128)}, f32[4,64,128]{2,1,0:T(8,128)}) custom-call(bf16[2,4,64,256]{3,2,1,0:T(8,128)(2,1)} %get-tuple-element.9.refs_0_, f32[64,128]{1,0:T(8,128)} %get-tuple-element.10.refs_1_, f32[4,64,128]{2,1,0:T(8,128)} %get-tuple-element.11.refs_2_), custom_call_target="tpu_custom_call" | custom-call | tf_op jit(solution)/shard_map/hand_over/pallas_call | solution.py:546
